TPU v7x, 128 devices: a whole 4x4x4 slice. The times are simulated.
128 devices in a mesh: wide: 32 (over y, z, core), narrow: 4 (over x).
Axes of the slice: x: 4, y: 4, z: 4, core: 2. Of those that a mesh axis runs over, the one named last changes fastest.
Arguments:
- superheat_excess: float32 [128, 512, 512], P('wide', 'narrow'), may hold values from -6 to 6
- liquid_indicator: int32 [128, 512, 512], P('wide', 'narrow'), may hold values from 0 to 1, as said below
- group_patch_listing_table: int32 [32, 4, 16], P('wide', 'narrow'), may hold values from -1 to 31, as said below
- source_smearing_factors_north: float32 [16, 16], replicated, may hold values from 0 to 2, as said below
- source_smearing_factors_east: float32 [128, 128], replicated, may hold values from 0 to 2, as said below
Outputs:
- temperature_next: float32 [128, 512, 512], P('wide', 'narrow')
- pressure: float32 [128, 512, 512], P('wide', 'narrow')
- residual: float32 [128, 512, 512], P('wide', 'narrow')
Inputs may be any that keep to these rules, and one draw needn't show every extreme that they name: In each row group_patch_listing_table[w, n] the listed tile numbers come first and are distinct, the remaining entries are -1. A row lists 1 to 16 tiles; for every w the rows n < 4 list exactly 32 tiles together, and one of them lists 16. `liquid_indicator`: phase is 1 in every cell outside the listed tiles. `source_smearing_factors_north`: the identity plus entries drawn in 0 to 1.2 / 16. `source_smearing_factors_east`: the identity plus entries drawn in 0 to 1.2 / 128.
All inputs are finite; a program needn't handle non-finite values.
Results may differ from a plain program's by a relative error of at most 0.0003.
Values sent between devices are 32-bit elements; how exact they have to be, the bound alone decides.
A program may use at most 64 MiB of HBM per device.

v0:
```python
import math

import jax
import jax.numpy as jnp
from jax import lax
from jax.sharding import Mesh
from jax.sharding import PartitionSpec as P

ITERS = 3
WIDE_NARROW = ("wide_0", "wide_1", "wide_2", "narrow")
WIDE = ("wide_0", "wide_1", "wide_2")


conduct_liquid = 1.0
conduct_vapor = 0.4
diffusion = 0.06
mobility_liquid = 1.0
mobility_vapor = 4.0
expansion = 0.3
compress = 0.01
highest = lax.Precision.HIGHEST


def padded_2(array, sides, width):
    edges = {}
    for axis, dim in sides:
        devices, length = (lax.axis_size(axis), array.shape[dim])
        up = [(i, (i + 1) % devices) for i in range(devices - 1)]
        last = lax.slice_in_dim(array, length - width, length, axis=dim)
        initial = lax.slice_in_dim(array, 0, width, axis=dim)
        edges[dim] = (
            lax.ppermute(last, axis, up),
            lax.ppermute(initial, axis, [(b, a) for a, b in up]),
        )
    done = []
    for _, dim in sides:
        low, high = edges[dim]
        around = [(width, width) if d in done else (0, 0) for d in range(array.ndim)]
        array = jnp.concatenate([jnp.pad(low, around), array, jnp.pad(high, around)], axis=dim)
        done.append(dim)
    return array


def over_axes(array, axes):
    for axis in axes:
        array = lax.psum(array, axis)
    return array


def centre(padded):
    return padded[1:-1, 1:-1, 1:-1]


def neighbours(padded):
    return [
        padded[2:, 1:-1, 1:-1],
        padded[:-2, 1:-1, 1:-1],
        padded[1:-1, 2:, 1:-1],
        padded[1:-1, :-2, 1:-1],
        padded[1:-1, 1:-1, 2:],
        padded[1:-1, 1:-1, :-2],
    ]


def heat_advance(temp_pad, liquid_indicator_haloed, inner_region_haloed):
    current = centre(temp_pad)
    phases = centre(liquid_indicator_haloed)
    conduct = jnp.where(phases > 0.5, conduct_liquid, conduct_vapor)
    flux = jnp.zeros_like(current)
    faces = jnp.zeros_like(current)
    for near_temp, near_phase, near_inside in zip(
        neighbours(temp_pad), neighbours(liquid_indicator_haloed), neighbours(inner_region_haloed)
    ):
        differ = jnp.abs(near_phase - phases) > 0.5
        flux = flux + near_inside * jnp.where(differ, -2.0 * current, near_temp - current)
        faces = faces + near_inside * jnp.where(differ, 1.0, 0.0)
    heated_values = current + diffusion * conduct * flux
    vaporised_amount = 2.0 * conduct * faces * heated_values
    return (heated_values, vaporised_amount)


def face_weights(liquid_indicator_haloed, inner_region_haloed):
    mobility = jnp.where(liquid_indicator_haloed > 0.5, mobility_liquid, mobility_vapor)
    own = centre(mobility)
    return [
        near_inside * 0.5 * (own + near_mob)
        for near_inside, near_mob in zip(neighbours(inner_region_haloed), neighbours(mobility))
    ]


def apply_operator(field_pad, weights):
    field = centre(field_pad)
    total = compress * field
    for weight, near in zip(weights, neighbours(field_pad)):
        total = total + weight * (field - near)
    return total


def smear_tiles(tiles, source_smearing_factors_north, source_smearing_factors_east):
    across = jnp.einsum("...bc,dc->...bd", tiles, source_smearing_factors_east, precision=highest)
    return expansion * jnp.einsum(
        "ab,...bd->...ad", source_smearing_factors_north, across, precision=highest
    )


def cosine_rows(extent, klength, clength):
    waves = jnp.arange(klength, dtype=jnp.int32)
    centres = 2 * jnp.arange(clength, dtype=jnp.int32) + 1
    turns = waves[:, None] * centres[None, :] % (4 * extent)
    angles = 2.0 * math.pi / (4 * extent) * turns.astype(jnp.float32)
    scales = jnp.where(waves == 0, math.sqrt(1.0 / extent), math.sqrt(2.0 / extent)).astype(
        jnp.float32
    )
    return scales[:, None] * jnp.cos(angles)


def eigen(extent, first, length):
    waves = (first + jnp.arange(length, dtype=jnp.int32)).astype(jnp.float32)
    return 4.0 * jnp.sin(waves * (math.pi / (2 * extent))) ** 2


def inside_range(first, length, limit):
    places = first + jnp.arange(length, dtype=jnp.int32)
    return jnp.logical_and(places >= 0, places < limit).astype(jnp.float32)


def padded_field(field):
    rimmed = padded_2(field, ((WIDE, 0), ("narrow", 1)), 1)
    return jnp.pad(rimmed, ((0, 0), (0, 0), (1, 1)))


def inner(first_field, second_field):
    return over_axes(jnp.sum(first_field * second_field), WIDE_NARROW)


def on_device(
    superheat_excess,
    liquid_indicator,
    group_patch_listing_table,
    source_smearing_factors_north,
    source_smearing_factors_east,
):
    sheet_thickness, north_line_total, patch_span_east = superheat_excess.shape
    wide_count = lax.axis_size(WIDE)
    lanes = lax.axis_size("narrow")
    wide_index = lax.axis_index(WIDE)
    lane_index = lax.axis_index("narrow")
    total_y = north_line_total * lanes
    total_z = sheet_thickness * wide_count
    gathered_patches = jnp.stack([superheat_excess, liquid_indicator.astype(jnp.float32)])
    rimmed = padded_2(gathered_patches, ((WIDE, 1), ("narrow", 2)), 1)
    rimmed = jnp.pad(rimmed, ((0, 0), (0, 0), (0, 0), (1, 1)))
    z_inside = inside_range(wide_index * sheet_thickness - 1, sheet_thickness + 2, total_z)
    y_inside = inside_range(lane_index * north_line_total - 1, north_line_total + 2, total_y)
    x_inside = inside_range(-1, patch_span_east + 2, patch_span_east)
    inner_region_haloed = (
        z_inside[:, None, None] * y_inside[None, :, None] * x_inside[None, None, :]
    )
    heated_values, vaporised_amount = heat_advance(rimmed[0], rimmed[1], inner_region_haloed)
    flat_ids = group_patch_listing_table.reshape(-1)
    most = flat_ids.shape[0]
    size_y = source_smearing_factors_north.shape[0]
    size_x = source_smearing_factors_east.shape[0]
    tiles_y = north_line_total // size_y
    tiles_x = patch_span_east // size_x
    count_tiles = tiles_y * tiles_x
    blocks = vaporised_amount.reshape(sheet_thickness, tiles_y, size_y, tiles_x, size_x).transpose(
        1, 3, 0, 2, 4
    )
    blocks = blocks.reshape(count_tiles, sheet_thickness * size_y * size_x)
    listed = flat_ids >= 0
    numbers = jnp.arange(count_tiles, dtype=jnp.int32)
    choose = jnp.logical_and(flat_ids[:, None] == numbers[None, :], listed[:, None]).astype(
        jnp.float32
    )
    picked = jnp.dot(choose, blocks, precision=highest)
    smeared = smear_tiles(
        picked.reshape(most, sheet_thickness, size_y, size_x),
        source_smearing_factors_north,
        source_smearing_factors_east,
    ).reshape(most, -1)
    sourced = jnp.dot(choose.T, smeared, precision=highest)
    source = sourced.reshape(tiles_y, tiles_x, sheet_thickness, size_y, size_x).transpose(
        2, 0, 3, 1, 4
    )
    source = source.reshape(sheet_thickness, north_line_total, patch_span_east)
    table_x = cosine_rows(patch_span_east, patch_span_east, patch_span_east)
    table_z = cosine_rows(total_z, total_z, total_z)
    eigen_z = eigen(total_z, 0, total_z)
    table_y = cosine_rows(total_y, total_y, total_y).reshape(total_y, lanes, north_line_total)
    table_zw = table_z.reshape(total_z, wide_count, sheet_thickness)
    part_k = patch_span_east // (wide_count * lanes)
    eigen_y = eigen(total_y, 0, total_y)
    eigen_x = eigen(patch_span_east, (wide_index * lanes + lane_index) * part_k, part_k)

    def precondition(remainder):
        spectrum = jnp.einsum("zyx,kx->zyk", remainder, table_x, precision=highest)
        planes = lax.all_to_all(
            spectrum[None], WIDE_NARROW, split_axis=3, concat_axis=0, tiled=True
        )
        planes = planes.reshape(wide_count, lanes, sheet_thickness, north_line_total, part_k)
        planes = jnp.einsum("wnzyk,mwz->mnyk", planes, table_zw, precision=highest)
        planes = jnp.einsum("mnyk,lny->mlk", planes, table_y, precision=highest)
        denom = eigen_z[:, None, None] + eigen_y[None, :, None] + eigen_x[None, None, :] + compress
        planes = jnp.einsum("mlk,lny->mnyk", planes / denom, table_y, precision=highest)
        planes = jnp.einsum("mnyk,mwz->wnzyk", planes, table_zw, precision=highest)
        planes = planes.reshape(wide_count * lanes, sheet_thickness, north_line_total, part_k)
        slabs = lax.all_to_all(planes, WIDE_NARROW, split_axis=0, concat_axis=3, tiled=True)
        return jnp.einsum("zyk,kx->zyx", slabs[0], table_x, precision=highest)

    weights = face_weights(rimmed[1], inner_region_haloed)
    pressure = jnp.zeros_like(source)
    residual = source
    search = precondition(residual)
    aligned = inner(residual, search)
    direction = search
    for iteration in range(ITERS):
        image = apply_operator(padded_field(direction), weights)
        alpha = aligned / over_axes(jnp.sum(direction * image), WIDE_NARROW)
        pressure = pressure + alpha * direction
        residual = residual - alpha * image
        if iteration + 1 < ITERS:
            search = precondition(residual)
            renewed = inner(residual, search)
            direction = search + renewed / aligned * direction
            aligned = renewed
    return (heated_values, pressure, residual)


def solution(mesh):
    torus = Mesh(
        mesh.devices.reshape(4, 4, 2, mesh.shape["narrow"]),
        ("wide_0", "wide_1", "wide_2", "narrow"),
    )
    placed = (P(WIDE, "narrow", None), P(WIDE, "narrow", None), P(WIDE, "narrow", None), P(), P())
    return jax.shard_map(
        on_device,
        mesh=torus,
        in_specs=placed,
        out_specs=(P(WIDE, "narrow", None), P(WIDE, "narrow", None), P(WIDE, "narrow", None)),
        check_vma=False,
    )
```

profile of v0, /device:TPU:0, one launch (start us, length us, event | category | flops | bytes accessed | tf_op | source)
XLA Modules:
  0.0 524.3 jit_solution(13043440437132954281)
XLA Ops:
  38.3 7.0 %convolution_bitcast_fusion.15 = f32[1,4,128,512]{3,2,1,0:T(8,128)} fusion(f32[4,128,512]{2,1,0:T(8,128)S(1)} %reshape.309, s32[512]{0:T(512)S(1)} %multiply_add_fusion.3, f32[512]{0:T(512)S(1)} %fusion.261), kind=kOutput, calls=%fused_computation.47 | convolution fusion | flops 1614544896 | bytes 2101248 | tf_op jit(solution)/shard_map/zyx,kx->zyk/dot_general | solution.py:197
  47.8 19.1 %all-to-all-start = ((f32[1,4,128,512]{2,1,0,3:T(4,128)}), f32[1,4,128,512]{2,1,0,3:T(4,128)S(1)}, u32[]{:S(2)}, u32[]{:S(2)}) async-start(f32[1,4,128,512]{2,1,0,3:T(4,128)} %copy.65), calls=%async_computation | async-start | bytes 2097152 | tf_op jit(solution)/shard_map/all_to_all | solution.py:198
  67.3 18.6 %all-to-all-done = f32[1,4,128,512]{2,1,0,3:T(4,128)S(1)} async-done(((f32[1,4,128,512]{2,1,0,3:T(4,128)}), f32[1,4,128,512]{2,1,0,3:T(4,128)S(1)}, u32[]{:S(2)}, u32[]{:S(2)}) %all-to-all-start) | async-done | bytes 1048608 | tf_op jit(solution)/shard_map/all_to_all | solution.py:198
  87.5 7.2 %convolution_bitcast_fusion.13 = f32[128,512,4]{0,1,2:T(8,128)S(1)} fusion(f32[128,4,128,4]{2,0,1,3:T(8,128)S(1)} %convolution_bitcast_fusion.14, s32[4,128]{1,0:T(4,128)S(1)} %multiply_add_fusion.4, f32[512]{0:T(512)S(1)} %fusion.261), kind=kOutput, calls=%fused_computation.45 | convolution fusion | flops 1614544896 | bytes 2101248 | tf_op jit(solution)/shard_map/mnyk,lny->mlk/dot_general | solution.py:203
  94.8 6.3 %convolution_bitcast_fusion.12 = f32[128,4,128,4,1]{0,2,3,1,4:T(8,128)S(1)} fusion(f32[128,512,4]{0,1,2:T(8,128)S(1)} %convolution_bitcast_fusion.13, f32[4]{0:T(128)S(1)} %multiply_multiply_fusion.1, f32[128,512]{0,1:T(8,128)S(1)} %broadcast_add_fusion, s32[4,128]{1,0:T(4,128)S(1)} %multiply_add_fusion.4, f32[512]{0:T(512)S(1)} %fusion.261), kind=kOutput, calls=%fused_computation.44 | convolution fusion | flops 1615331328 | bytes 2363408 | tf_op jit(solution)/shard_map/mlk,lny->mnyk/dot_general | solution.py:205
  103.8 23.1 %all_to_all.90 = f32[128,4,128,4]{2,3,1,0:T(4,128)S(1)} all-to-all(f32[128,4,128,4]{2,3,1,0:T(4,128)S(1)} %copy.74), channel_id=1, replica_groups=mesh['wide_0'=4,'wide_1'=4,'wide_2'=2,'narrow'=4] {'wide_0','wide_1','wi..., dimensions={0} | all-to-all | bytes 2097152 | tf_op jit(solution)/shard_map/all_to_all | solution.py:208
  145.3 7.6 %multiply_reduce_fusion.4 = (f32[]{:T(128)}, f32[]{:T(128)}, f32[4,128,512]{2,1,0:T(8,128)}, f32[4,128,512]{2,1,0:T(8,128)}, f32[4,128,512]{2,1,0:T(8,128)}, /*i...) fusion(f32[4,128,512]{2,1,0:T(8,128)S(1)} %fusion.126, ...), kind=kLoop, calls=%fused_computation.222 | loop fusion | flops 12845054 | bytes 25714696 | tf_op jit(solution)/shard_map/reduce_sum | solution.py:219
  152.9 13.7 %all-reduce.14 = (f32[]{:T(128)}, f32[]{:T(128)}) all-reduce(f32[]{:T(128)} %get-tuple-element.4, f32[]{:T(128)} %get-tuple-element.3), channel_id=1, replica_groups=mesh['wide_0'=4,'wide_1'=4,'wide_2'=2,'narrow'=4] {'wide_0'}, use_global_device_ids=true, to_apply=%region_1.2 | all-reduce | flops 2 | bytes 16 | tf_op jit(solution)/shard_map/psum | solution.py:46
  166.6 8.4 %all-reduce.13 = (f32[]{:T(128)}, f32[]{:T(128)}) all-reduce(f32[]{:T(128)} %get-tuple-element.9, f32[]{:T(128)} %get-tuple-element.10), channel_id=1, replica_groups=mesh['wide_0'=4,'wide_1'=4,'wide_2'=2,'narrow'=4] {'wide_1'}, use_global_device_ids=true, to_apply=%region_2.3 | all-reduce | flops 2 | bytes 16 | tf_op jit(solution)/shard_map/psum | solution.py:46
  178.1 9.1 %all-reduce.12 = (f32[]{:T(128)}, f32[]{:T(128)}) all-reduce(f32[]{:T(128)} %get-tuple-element.11, f32[]{:T(128)} %get-tuple-element.12), channel_id=1, replica_groups=mesh['wide_0'=4,'wide_1'=4,'wide_2'=2,'narrow'=4] {'narrow'}, use_global_device_ids=true, to_apply=%region_4.5 | all-reduce | flops 2 | bytes 16 | tf_op jit(solution)/shard_map/psum | solution.py:46
  190.3 6.8 %convolution_bitcast_fusion.10 = f32[1,4,128,512]{3,2,1,0:T(8,128)} fusion(f32[4,128,512]{2,1,0:T(8,128)S(1)} %multiply_subtract_fusion.2, s32[512]{0:T(512)S(1)} %multiply_add_fusion.3, f32[512]{0:T(512)S(1)} %fusion.261), kind=kOutput, calls=%fused_computation.42 | convolution fusion | flops 1614544896 | bytes 2101248 | tf_op jit(solution)/shard_map/zyx,kx->zyk/dot_general | solution.py:197
  198.7 23.7 %all_to_all.91 = f32[1,4,128,512]{2,1,0,3:T(4,128)S(1)} all-to-all(f32[1,4,128,512]{2,1,0,3:T(4,128)S(1)} %copy.77), channel_id=1, replica_groups=mesh['wide_0'=4,'wide_1'=4,'wide_2'=2,'narrow'=4] {'wide_0','wide_1','wi..., dimensions={3} | all-to-all | bytes 2097152 | tf_op jit(solution)/shard_map/all_to_all | solution.py:198
  224.0 7.2 %convolution_bitcast_fusion.8 = f32[128,512,4]{0,1,2:T(8,128)S(1)} fusion(f32[128,4,128,4]{2,0,1,3:T(8,128)S(1)} %convolution_bitcast_fusion.9, s32[4,128]{1,0:T(4,128)S(1)} %multiply_add_fusion.4, f32[512]{0:T(512)S(1)} %fusion.261), kind=kOutput, calls=%fused_computation.40 | convolution fusion | flops 1614544896 | bytes 2101248 | tf_op jit(solution)/shard_map/mnyk,lny->mlk/dot_general | solution.py:203
  240.0 22.9 %all_to_all.92 = f32[128,4,128,4]{2,3,1,0:T(4,128)S(1)} all-to-all(f32[128,4,128,4]{2,3,1,0:T(4,128)S(1)} %copy.86), channel_id=1, replica_groups=mesh['wide_0'=4,'wide_1'=4,'wide_2'=2,'narrow'=4] {'wide_0','wide_1','wi..., dimensions={0} | all-to-all | bytes 2097152 | tf_op jit(solution)/shard_map/all_to_all | solution.py:208
  263.1 6.6 %multiply_reduce_fusion.3 = (f32[]{:T(128)}, f32[4,128,512]{2,1,0:T(8,128)S(1)}) fusion(f32[4,128,512]{2,1,0:T(8,128)S(1)} %multiply_subtract_fusion.2, f32[4,128,512]{1,2,0:T(8,128)S(1)} %bitcast.220, s32[512]{0:T(512)S(1)} %multiply_add_fusion.3, f32[512]{0:T(512)S(1)} %fusion.261), kind=kOutput, calls=%fused_computation.219 | convolution fusion | flops 1615069184 | bytes 3149828 | tf_op jit(solution)/shard_map/zyk,kx->zyx/dot_general | solution.py:209
  269.7 9.5 %psum.176 = f32[]{:T(128)} all-reduce(f32[]{:T(128)} %get-tuple-element.51), channel_id=1, replica_groups=mesh['wide_0'=4,'wide_1'=4,'wide_2'=2,'narrow'=4] {'wide_0'}, use_global_device_ids=true, to_apply=%region_11.12 | all-reduce | flops 1 | bytes 8 | tf_op jit(solution)/shard_map/psum | solution.py:46
  279.2 9.2 %psum.177 = f32[]{:T(128)} all-reduce(f32[]{:T(128)} %psum.176), channel_id=1, replica_groups=mesh['wide_0'=4,'wide_1'=4,'wide_2'=2,'narrow'=4] {'wide_1'}, use_global_device_ids=true, to_apply=%region_12.13 | all-reduce | flops 1 | bytes 8 | tf_op jit(solution)/shard_map/psum | solution.py:46
  291.4 9.2 %psum.179 = f32[]{:T(128)} all-reduce(f32[]{:T(128)} %psum.178), channel_id=1, replica_groups=mesh['wide_0'=4,'wide_1'=4,'wide_2'=2,'narrow'=4] {'narrow'}, use_global_device_ids=true, to_apply=%region_14.15 | all-reduce | flops 1 | bytes 8 | tf_op jit(solution)/shard_map/psum | solution.py:46
  316.7 14.3 %psum.180 = f32[]{:T(128)} all-reduce(f32[]{:T(128)} %get-tuple-element.15), channel_id=1, replica_groups=mesh['wide_0'=4,'wide_1'=4,'wide_2'=2,'narrow'=4] {'wide_0'}, use_global_device_ids=true, to_apply=%region_16.17 | all-reduce | flops 1 | bytes 8 | tf_op jit(solution)/shard_map/psum | solution.py:46
  331.1 8.3 %psum.181 = f32[]{:T(128)} all-reduce(f32[]{:T(128)} %psum.180), channel_id=1, replica_groups=mesh['wide_0'=4,'wide_1'=4,'wide_2'=2,'narrow'=4] {'wide_1'}, use_global_device_ids=true, to_apply=%region_17.18 | all-reduce | flops 1 | bytes 8 | tf_op jit(solution)/shard_map/psum | solution.py:46
  342.5 8.4 %psum.183 = f32[]{:T(128)} all-reduce(f32[]{:T(128)} %psum.182), channel_id=1, replica_groups=mesh['wide_0'=4,'wide_1'=4,'wide_2'=2,'narrow'=4] {'narrow'}, use_global_device_ids=true, to_apply=%region_19.20 | all-reduce | flops 1 | bytes 8 | tf_op jit(solution)/shard_map/psum | solution.py:46
  354.5 6.8 %convolution_bitcast_fusion.5 = f32[1,4,128,512]{3,2,1,0:T(8,128)} fusion(f32[4,128,512]{2,1,0:T(8,128)S(1)} %multiply_subtract_fusion.1, s32[512]{0:T(512)S(1)} %multiply_add_fusion.3, f32[512]{0:T(512)S(1)} %fusion.261), kind=kOutput, calls=%fused_computation.37 | convolution fusion | flops 1614544896 | bytes 2101248 | tf_op jit(solution)/shard_map/zyx,kx->zyk/dot_general | solution.py:197
  362.9 24.4 %all_to_all.93 = f32[1,4,128,512]{2,1,0,3:T(4,128)S(1)} all-to-all(f32[1,4,128,512]{2,1,0,3:T(4,128)S(1)} %copy.89), channel_id=1, replica_groups=mesh['wide_0'=4,'wide_1'=4,'wide_2'=2,'narrow'=4] {'wide_0','wide_1','wi..., dimensions={3} | all-to-all | bytes 2097152 | tf_op jit(solution)/shard_map/all_to_all | solution.py:198
  389.0 7.2 %convolution_bitcast_fusion.3 = f32[128,512,4]{0,1,2:T(8,128)S(1)} fusion(f32[128,4,128,4]{2,0,1,3:T(8,128)S(1)} %convolution_bitcast_fusion.4, s32[4,128]{1,0:T(4,128)S(1)} %multiply_add_fusion.4, f32[512]{0:T(512)S(1)} %fusion.261), kind=kOutput, calls=%fused_computation.35 | convolution fusion | flops 1614544896 | bytes 2101248 | tf_op jit(solution)/shard_map/mnyk,lny->mlk/dot_general | solution.py:203
  405.0 23.0 %all_to_all.94 = f32[128,4,128,4]{2,3,1,0:T(4,128)S(1)} all-to-all(f32[128,4,128,4]{2,3,1,0:T(4,128)S(1)} %copy.98), channel_id=1, replica_groups=mesh['wide_0'=4,'wide_1'=4,'wide_2'=2,'narrow'=4] {'wide_0','wide_1','wi..., dimensions={0} | all-to-all | bytes 2097152 | tf_op jit(solution)/shard_map/all_to_all | solution.py:208
  428.3 7.5 %multiply_reduce_fusion.1 = (f32[]{:T(128)}, f32[4,128,512]{2,1,0:T(8,128)}) fusion(f32[4,128,512]{2,1,0:T(8,128)S(1)} %copy-done.21, f32[4,128,512]{1,2,0:T(8,128)S(1)} %bitcast.219, s32[512]{0:T(512)S(1)} %multiply_add_fusion.3, f32[512]{0:T(512)S(1)} %fusion.261), kind=kOutput, calls=%fused_computation.214 | convolution fusion | flops 1615069184 | bytes 3149828 | tf_op jit(solution)/shard_map/zyk,kx->zyx/dot_general | solution.py:209
  435.8 9.5 %psum.184 = f32[]{:T(128)} all-reduce(f32[]{:T(128)} %get-tuple-element.53), channel_id=1, replica_groups=mesh['wide_0'=4,'wide_1'=4,'wide_2'=2,'narrow'=4] {'wide_0'}, use_global_device_ids=true, to_apply=%region_21.22 | all-reduce | flops 1 | bytes 8 | tf_op jit(solution)/shard_map/psum | solution.py:46
  445.3 9.2 %psum.185 = f32[]{:T(128)} all-reduce(f32[]{:T(128)} %psum.184), channel_id=1, replica_groups=mesh['wide_0'=4,'wide_1'=4,'wide_2'=2,'narrow'=4] {'wide_1'}, use_global_device_ids=true, to_apply=%region_22.23 | all-reduce | flops 1 | bytes 8 | tf_op jit(solution)/shard_map/psum | solution.py:46
  457.7 9.2 %psum.187 = f32[]{:T(128)} all-reduce(f32[]{:T(128)} %psum.186), channel_id=1, replica_groups=mesh['wide_0'=4,'wide_1'=4,'wide_2'=2,'narrow'=4] {'narrow'}, use_global_device_ids=true, to_apply=%region_24.25 | all-reduce | flops 1 | bytes 8 | tf_op jit(solution)/shard_map/psum | solution.py:46
  485.3 14.3 %psum.188 = f32[]{:T(128)} all-reduce(f32[]{:T(128)} %get-tuple-element.13), channel_id=1, replica_groups=mesh['wide_0'=4,'wide_1'=4,'wide_2'=2,'narrow'=4] {'wide_0'}, use_global_device_ids=true, to_apply=%region_26.27 | all-reduce | flops 1 | bytes 8 | tf_op jit(solution)/shard_map/psum | solution.py:46
  499.6 8.3 %psum.189 = f32[]{:T(128)} all-reduce(f32[]{:T(128)} %psum.188), channel_id=1, replica_groups=mesh['wide_0'=4,'wide_1'=4,'wide_2'=2,'narrow'=4] {'wide_1'}, use_global_device_ids=true, to_apply=%region_27.28 | all-reduce | flops 1 | bytes 8 | tf_op jit(solution)/shard_map/psum | solution.py:46
  511.0 8.3 %psum.191 = f32[]{:T(128)} all-reduce(f32[]{:T(128)} %psum.190), channel_id=1, replica_groups=mesh['wide_0'=4,'wide_1'=4,'wide_2'=2,'narrow'=4] {'narrow'}, use_global_device_ids=true, to_apply=%region_29.30 | all-reduce | flops 1 | bytes 8 | tf_op jit(solution)/shard_map/psum | solution.py:46
  (167 shorter events, 142.4 us)
Async XLA Ops:
  0.6 31.8 %copy-start = (f32[128,128]{1,0:T(8,128)S(1)}, f32[128,128]{1,0:T(8,128)}, u32[]{:S(2)}) copy-start(f32[128,128]{1,0:T(8,128)} %param.9) | copy-start | bytes 196612
  2.3 9.8 %collective-permute-start = (f32[2,4,1,512]{3,2,1,0:T(1,128)S(1)}, f32[2,4,1,512]{3,2,1,0:T(1,128)S(1)}, u32[]{:S(2)}, u32[]{:S(2)}) collective-permute-start(f32[2,4,1,512]{3,2,1,0:T(1,128)S(1)} %get-tuple-element.30), channel_id=1, source_target_pairs={{0,1},{1,2},{2,3},{4,5},{5,6},{6,7},{8,9},{9,10},{10,11},{12,13},{... | collective-permute-start | bytes 49160 | tf_op jit(solution)/shard_map/ppermute | solution.py:32
  5.7 6.3 %collective-permute-start.3 = (f32[2,4,1,512]{3,2,1,0:T(1,128)S(1)}, f32[2,4,1,512]{3,2,1,0:T(1,128)S(1)}, u32[]{:S(2)}, u32[]{:S(2)}) collective-permute-start(f32[2,4,1,512]{3,2,1,0:T(1,128)S(1)} %get-tuple-element.31), channel_id=1, source_target_pairs={{1,0},{2,1},{3,2},{5,4},{6,5},{7,6},{9,8},{10,9},{11,10},{13,12},{... | collective-permute-start | bytes 49160 | tf_op jit(solution)/shard_map/ppermute | solution.py:33
  8.1 4.0 collective-permute-start.1
  10.4 5.3 %collective-permute-start.2 = (f32[2,1,128,512]{3,2,1,0:T(8,128)}, f32[2,1,128,512]{3,2,1,0:T(8,128)}, u32[]{:S(2)}, u32[]{:S(2)}) collective-permute-start(f32[2,1,128,512]{3,2,1,0:T(8,128)} %get-tuple-element.29), channel_id=1, source_target_pairs={{4,0},{8,4},{12,8},{16,12},{20,16},{24,20},{28,24},{32,28},{36,32}... | collective-permute-start | bytes 1572872 | tf_op jit(solution)/shard_map/ppermute | solution.py:33
  47.8 38.0 %all-to-all-start = ((f32[1,4,128,512]{2,1,0,3:T(4,128)}), f32[1,4,128,512]{2,1,0,3:T(4,128)S(1)}, u32[]{:S(2)}, u32[]{:S(2)}) async-start(f32[1,4,128,512]{2,1,0,3:T(4,128)} %copy.65), calls=%async_computation | async-start | bytes 2097152 | tf_op jit(solution)/shard_map/all_to_all | solution.py:198
  127.0 13.2 %copy-start.3 = (f32[2,6,130,512]{3,2,1,0:T(8,128)S(1)}, f32[2,6,130,512]{3,2,1,0:T(8,128)}, u32[]{:S(2)}) copy-start(f32[2,6,130,512]{3,2,1,0:T(8,128)} %copy-done.2) | copy-start | bytes 9584644
  132.9 11.6 %collective-permute-start.5 = (f32[1,128,512]{2,1,0:T(8,128)S(1)}, f32[1,128,512]{2,1,0:T(8,128)S(1)}, u32[]{:S(2)}, u32[]{:S(2)}) collective-permute-start(f32[1,128,512]{2,1,0:T(8,128)S(1)} %get-tuple-element.47), channel_id=1, source_target_pairs={{0,4},{4,8},{8,12},{12,16},{16,20},{20,24},{24,28},{28,32},{32,36}... | collective-permute-start | bytes 786440 | tf_op jit(solution)/shard_map/ppermute | solution.py:32
  135.1 9.5 %collective-permute-start.4 = (f32[1,128,512]{2,1,0:T(8,128)S(1)}, f32[1,128,512]{2,1,0:T(8,128)S(1)}, u32[]{:S(2)}, u32[]{:S(2)}) collective-permute-start(f32[1,128,512]{2,1,0:T(8,128)S(1)} %get-tuple-element.48), channel_id=1, source_target_pairs={{4,0},{8,4},{12,8},{16,12},{20,16},{24,20},{28,24},{32,28},{36,32}... | collective-permute-start | bytes 786440 | tf_op jit(solution)/shard_map/ppermute | solution.py:33
  136.5 4.4 collective-permute-start.7
  139.0 5.6 %collective-permute-start.6 = (f32[4,1,512]{2,1,0:T(1,128)S(1)}, f32[4,1,512]{2,1,0:T(1,128)S(1)}, u32[]{:S(2)}, u32[]{:S(2)}) collective-permute-start(f32[4,1,512]{2,1,0:T(1,128)S(1)} %get-tuple-element.50), channel_id=1, source_target_pairs={{1,0},{2,1},{3,2},{5,4},{6,5},{7,6},{9,8},{10,9},{11,10},{13,12},{... | collective-permute-start | bytes 24584 | tf_op jit(solution)/shard_map/ppermute | solution.py:33
  190.2 72.9 %copy-start.19 = (f32[4,128,512]{2,1,0:T(8,128)}, f32[4,128,512]{2,1,0:T(8,128)S(1)}, u32[]{:S(2)}) copy-start(f32[4,128,512]{2,1,0:T(8,128)S(1)} %multiply_subtract_fusion.2) | copy-start | bytes 3145732
  301.8 12.7 %copy-start.13 = (f32[4,128,512]{2,1,0:T(8,128)S(1)}, f32[4,128,512]{2,1,0:T(8,128)}, u32[]{:S(2)}) copy-start(f32[4,128,512]{2,1,0:T(8,128)} %get-tuple-element.22) | copy-start | bytes 3145732
  301.8 12.7 %copy-start.15 = (f32[4,128,512]{2,1,0:T(8,128)S(1)}, f32[4,128,512]{2,1,0:T(8,128)}, u32[]{:S(2)}) copy-start(f32[4,128,512]{2,1,0:T(8,128)} %get-tuple-element.23) | copy-start | bytes 3145732
  302.1 12.4 %copy-start.11 = (f32[4,128,512]{2,1,0:T(8,128)S(1)}, f32[4,128,512]{2,1,0:T(8,128)}, u32[]{:S(2)}) copy-start(f32[4,128,512]{2,1,0:T(8,128)} %get-tuple-element.21) | copy-start | bytes 3145732
  302.1 12.4 %copy-start.5 = (f32[4,128,512]{2,1,0:T(8,128)S(1)}, f32[4,128,512]{2,1,0:T(8,128)}, u32[]{:S(2)}) copy-start(f32[4,128,512]{2,1,0:T(8,128)} %get-tuple-element.18) | copy-start | bytes 3145732
  302.1 12.4 %copy-start.7 = (f32[4,128,512]{2,1,0:T(8,128)S(1)}, f32[4,128,512]{2,1,0:T(8,128)}, u32[]{:S(2)}) copy-start(f32[4,128,512]{2,1,0:T(8,128)} %get-tuple-element.19) | copy-start | bytes 3145732
  302.1 11.6 %collective-permute-start.9 = (f32[1,128,512]{2,1,0:T(8,128)S(1)}, f32[1,128,512]{2,1,0:T(8,128)S(1)}, u32[]{:S(2)}, u32[]{:S(2)}) collective-permute-start(f32[1,128,512]{2,1,0:T(8,128)S(1)} %get-tuple-element.43), channel_id=1, source_target_pairs={{0,4},{4,8},{8,12},{12,16},{16,20},{20,24},{24,28},{28,32},{32,36}... | collective-permute-start | bytes 786440 | tf_op jit(solution)/shard_map/ppermute | solution.py:32
  303.7 10.0 %collective-permute-start.8 = (f32[1,128,512]{2,1,0:T(8,128)S(1)}, f32[1,128,512]{2,1,0:T(8,128)S(1)}, u32[]{:S(2)}, u32[]{:S(2)}) collective-permute-start(f32[1,128,512]{2,1,0:T(8,128)S(1)} %get-tuple-element.44), channel_id=1, source_target_pairs={{4,0},{8,4},{12,8},{16,12},{20,16},{24,20},{28,24},{32,28},{36,32}... | collective-permute-start | bytes 786440 | tf_op jit(solution)/shard_map/ppermute | solution.py:33
  305.0 4.5 collective-permute-start.11
  308.1 5.5 %collective-permute-start.10 = (f32[4,1,512]{2,1,0:T(1,128)S(1)}, f32[4,1,512]{2,1,0:T(1,128)S(1)}, u32[]{:S(2)}, u32[]{:S(2)}) collective-permute-start(f32[4,1,512]{2,1,0:T(1,128)S(1)} %get-tuple-element.46), channel_id=1, source_target_pairs={{1,0},{2,1},{3,2},{5,4},{6,5},{7,6},{9,8},{10,9},{11,10},{13,12},{... | collective-permute-start | bytes 24584 | tf_op jit(solution)/shard_map/ppermute | solution.py:33
  405.0 23.2 %copy-start.21 = (f32[4,128,512]{2,1,0:T(8,128)S(1)}, f32[4,128,512]{2,1,0:T(8,128)}, u32[]{:S(2)}) copy-start(f32[4,128,512]{2,1,0:T(8,128)} %copy-done.20) | copy-start | bytes 3145732
  468.1 14.0 %copy-start.14 = (f32[4,128,512]{2,1,0:T(8,128)S(1)}, f32[4,128,512]{2,1,0:T(8,128)}, u32[]{:S(2)}) copy-start(f32[4,128,512]{2,1,0:T(8,128)} %get-tuple-element.22) | copy-start | bytes 3145732
  468.1 14.0 %copy-start.16 = (f32[4,128,512]{2,1,0:T(8,128)S(1)}, f32[4,128,512]{2,1,0:T(8,128)}, u32[]{:S(2)}) copy-start(f32[4,128,512]{2,1,0:T(8,128)} %get-tuple-element.23) | copy-start | bytes 3145732
  469.7 12.4 %copy-start.12 = (f32[4,128,512]{2,1,0:T(8,128)S(1)}, f32[4,128,512]{2,1,0:T(8,128)}, u32[]{:S(2)}) copy-start(f32[4,128,512]{2,1,0:T(8,128)} %get-tuple-element.21) | copy-start | bytes 3145732
  469.8 12.4 %copy-start.6 = (f32[4,128,512]{2,1,0:T(8,128)S(1)}, f32[4,128,512]{2,1,0:T(8,128)}, u32[]{:S(2)}) copy-start(f32[4,128,512]{2,1,0:T(8,128)} %get-tuple-element.18) | copy-start | bytes 3145732
  469.8 12.4 %copy-start.8 = (f32[4,128,512]{2,1,0:T(8,128)S(1)}, f32[4,128,512]{2,1,0:T(8,128)}, u32[]{:S(2)}) copy-start(f32[4,128,512]{2,1,0:T(8,128)} %get-tuple-element.19) | copy-start | bytes 3145732
  469.8 12.4 %copy-start.10 = (f32[4,128,512]{2,1,0:T(8,128)S(1)}, f32[4,128,512]{2,1,0:T(8,128)}, u32[]{:S(2)}) copy-start(f32[4,128,512]{2,1,0:T(8,128)} %get-tuple-element.20) | copy-start | bytes 3145732
  469.8 11.6 %collective-permute-start.13 = (f32[1,128,512]{2,1,0:T(8,128)S(1)}, f32[1,128,512]{2,1,0:T(8,128)S(1)}, u32[]{:S(2)}, u32[]{:S(2)}) collective-permute-start(f32[1,128,512]{2,1,0:T(8,128)S(1)} %get-tuple-element.39), channel_id=1, source_target_pairs={{0,4},{4,8},{8,12},{12,16},{16,20},{20,24},{24,28},{28,32},{32,36}... | collective-permute-start | bytes 786440 | tf_op jit(solution)/shard_map/ppermute | solution.py:32
  471.4 10.0 %collective-permute-start.12 = (f32[1,128,512]{2,1,0:T(8,128)S(1)}, f32[1,128,512]{2,1,0:T(8,128)S(1)}, u32[]{:S(2)}, u32[]{:S(2)}) collective-permute-start(f32[1,128,512]{2,1,0:T(8,128)S(1)} %get-tuple-element.40), channel_id=1, source_target_pairs={{4,0},{8,4},{12,8},{16,12},{20,16},{24,20},{28,24},{32,28},{36,32}... | collective-permute-start | bytes 786440 | tf_op jit(solution)/shard_map/ppermute | solution.py:33
  472.7 4.5 collective-permute-start.15
  475.8 5.5 %collective-permute-start.14 = (f32[4,1,512]{2,1,0:T(1,128)S(1)}, f32[4,1,512]{2,1,0:T(1,128)S(1)}, u32[]{:S(2)}, u32[]{:S(2)}) collective-permute-start(f32[4,1,512]{2,1,0:T(1,128)S(1)} %get-tuple-element.42), channel_id=1, source_target_pairs={{1,0},{2,1},{3,2},{5,4},{6,5},{7,6},{9,8},{10,9},{11,10},{13,12},{... | collective-permute-start | bytes 24584 | tf_op jit(solution)/shard_map/ppermute | solution.py:33
  (9 other events, 44.2 us)
where the time goes:
time: 535 us; the launch traced here: 524 us
  blocking collectives  281 us (53%)
  matrix products  92.4 us (17%)
  starting transfers between devices  49.2 us (9%)
  other arithmetic  36.1 us (7%)
  waiting for transfers between devices  34.3 us (6%)
  local copies, waits for them, and re-layouts  22.7 us (4%)
  between operations  8.12 us (2%)
    psum x20, blocking collectives, over_axes(): array = lax.psum(array, axis)  164 us
    all_to_all x3, blocking collectives, precondition(): lax.all_to_all(planes, WIDE_NARROW, split_axis=0, concat_axis=3, tiled=True)  69 us
    all_to_all x2, blocking collectives, precondition(): lax.all_to_all(spectrum[None], WIDE_NARROW, split_axis=3, concat_axis=0,...  48.1 us
    dot_general x3, matrix products, precondition(): planes = jnp.einsum('mnyk,lny->mlk', planes, table_y, precision=highest)  21.7 us
    dot_general x3, matrix products, precondition(): spectrum = jnp.einsum('zyx,kx->zyk', remainder, table_x, precision=highest)  20.5 us
    dot_general x3, matrix products, precondition(): return jnp.einsum('zyk,kx->zyx', slabs[0], table_x, precision=highest)  19.9 us
    ppermute x8, starting transfers between devices, padded_2(): lax.ppermute(last, axis, up)  19.8 us
    all_to_all x1, starting transfers between devices, precondition(): lax.all_to_all(spectrum[None], WIDE_NARROW, split_axis=3, concat_axis=0,...  19.1 us
  transfers between devices with their start and end apart: 17, of which 5 were waited for; matrix products, arithmetic and copies ran while one was open for 0% of the time, Pallas kernels for 0%

commit v1 on v0

v1 whole, which is shorter than its diff:
```python
import functools
import math

import jax
import jax.numpy as jnp
import ml_dtypes
import numpy as np
from jax import lax
from jax.experimental import pallas as pl
from jax.experimental.pallas import tpu as pltpu
from jax.sharding import PartitionSpec as P

MESH = pl.DeviceIdType.MESH
F32 = jnp.float32
BF16 = jnp.bfloat16
NX, NY, NZ = 512, 512, 128
NW, NN = 32, 4
ND = NW * NN
ITERS = 3
ROWS = 512
FWD, INV = 3, 3


def cosine_np(m):
    k = np.arange(m)[:, None]
    i = np.arange(m)[None, :]
    scale = np.where(k == 0, math.sqrt(1.0 / m), math.sqrt(2.0 / m))
    return scale * np.cos(np.pi * ((k * (2 * i + 1)) % (4 * m)) / (2 * m))


def eigen_np(m):
    return 4.0 * np.sin(np.pi * np.arange(m) / (2 * m)) ** 2


def split_np(table):
    parts = []
    rest = table.astype(np.float64)
    for _ in range(3):
        part = rest.astype(np.float32).astype(ml_dtypes.bfloat16)
        parts.append(part)
        rest = rest - part.astype(np.float64)
    return np.stack(parts)


def z_table():
    table = cosine_np(NZ).reshape(NZ, NW, 2, 2).transpose(0, 3, 1, 2)
    big = np.zeros((NZ, 4, 2, NW, 2, 4))
    for k in range(4):
        big[:, k, :, :, :, k] = table
    return big.reshape(ROWS, ROWS)


def split(x, parts):
    out = []
    for i in range(parts):
        part = x.astype(BF16)
        out.append(part)
        if i + 1 < parts:
            x = x - part.astype(F32)
    return out


PAIRS = {3: ((0, 1), (1, 0), (0, 0)), 6: ((1, 1), (0, 2), (2, 0), (0, 1), (1, 0), (0, 0))}


def product(a, b, dims, passes):
    total = None
    for i, j in PAIRS[passes]:
        term = lax.dot_general(a[i], b[j], (dims, ((), ())), preferred_element_type=F32)
        total = term if total is None else total + term
    return total


def peer(step, w, n):
    dx, dy, dz, dc = step % 4, (step // 4) % 4, (step // 16) % 4, step // 64
    y, z, c = w // 8, (w // 2) % 4, w % 2
    return ((y + dy) % 4) * 8 + ((z + dz) % 4) * 2 + (c + dc) % 2, (n + dx) % 4


def whole_kernel(
    temp_ref, phase_ref, table_ref, north_ref, east_ref, tx_ref, ty_ref, b_ref, bt_ref, rowden_ref, colden_ref,
    tnext_ref, press_ref, resid_ref,
    tpad, ppad, spad, wts, mass, f_ref, c_ref, d_ref, inv_ref,
    sbf, sbi, recvf, recvi, ag_a, ag_b,
    sem_fs, sem_fr, sem_is, sem_ir, sem_as, sem_ar, sem_bs, sem_br, sem_hs, sem_hr,
):
    w = lax.axis_index("wide")
    n = lax.axis_index("narrow")
    me = n * NW + w

    barrier = pltpu.get_barrier_semaphore()

    def greet(step, carry):
        pw, pn = peer(step, w, n)
        pl.semaphore_signal(barrier, inc=1, device_id=(pw, pn), device_id_type=MESH)
        return carry

    lax.fori_loop(1, ND, greet, 0)

    tpad[1:5, 8:136, :] = temp_ref[...]
    ppad[1:5, 8:136, :] = phase_ref[...]
    inv_ref[...] = 1.0 / (rowden_ref[...] + colden_ref[...])
    c_ref[...] = jnp.zeros_like(c_ref)
    d_ref[...] = jnp.zeros_like(d_ref)
    press_ref[...] = jnp.zeros_like(press_ref)
    ag_a[0, me] = jnp.ones((1, 128), F32)

    pl.semaphore_wait(barrier, ND - 1)

    w_up, w_down = (w + 1) % NW, (w + NW - 1) % NW
    n_up, n_down = (n + 1) % NN, (n + NN - 1) % NN

    def halo(slot, src, at, dst):
        moves = (
            (src(3, pl.ds(at, 128)), dst(0, pl.ds(8, 128)), (w_up, n)),
            (src(0, pl.ds(at, 128)), dst(5, pl.ds(8, 128)), (w_down, n)),
            (src(pl.ds(0, 4), pl.ds(at + 120, 8)), dst(pl.ds(1, 4), pl.ds(0, 8)), (w, n_up)),
            (src(pl.ds(0, 4), pl.ds(at, 8)), dst(pl.ds(1, 4), pl.ds(136, 8)), (w, n_down)),
        )
        copies = []
        for i, (a, b, to) in enumerate(moves):
            copies.append(
                pltpu.make_async_remote_copy(
                    src_ref=a,
                    dst_ref=b,
                    send_sem=sem_hs.at[slot, i],
                    recv_sem=sem_hr.at[slot, i],
                    device_id=to,
                    device_id_type=MESH,
                )
            )
        return copies

    head = halo(0, lambda z, y: temp_ref.at[z, y], 0, lambda z, y: tpad.at[z, y])
    head += halo(1, lambda z, y: phase_ref.at[z, y], 0, lambda z, y: ppad.at[z, y])
    for copy in head:
        copy.start()
    for copy in head:
        copy.wait()

    row8 = lax.broadcasted_iota(jnp.int32, (8, NX), 0)
    lane8 = lax.broadcasted_iota(jnp.int32, (8, NX), 1)

    def around(pad, z, i):
        mid = pl.ds(pl.multiple_of(8 + 8 * i, 8), 8)
        low = pl.ds(pl.multiple_of(8 * i, 8), 8)
        high = pl.ds(pl.multiple_of(16 + 8 * i, 8), 8)
        c = pad[z + 1, mid, :]
        up = pad[z + 1, high, :]
        down = pad[z + 1, low, :]
        near = (
            pad[z + 2, mid, :],
            pad[z, mid, :],
            pltpu.roll(jnp.where(row8 == 0, up, c), 7, 0),
            pltpu.roll(jnp.where(row8 == 7, down, c), 1, 0),
            pltpu.roll(c, NX - 1, 1),
            pltpu.roll(c, 1, 1),
        )
        return c, near

    def head_chunk(g, carry):
        z, i = g // 16, g % 16
        rows = pl.ds(pl.multiple_of(8 * g, 8), 8)
        c, near = around(tpad, z, i)
        pc, pnear = around(ppad, z, i)
        gz = jnp.zeros_like(row8) + (4 * w + z)
        gy = row8 + (n * 128 + 8 * i)
        inside = (gz < NZ - 1, gz > 0, gy < NY - 1, gy > 0, lane8 < NX - 1, lane8 > 0)
        conduct = jnp.where(pc > 0, 1.0, 0.4)
        beta = jnp.where(pc > 0, 1.0, 4.0)
        flux = jnp.zeros_like(c)
        faces = jnp.zeros_like(c)
        for q in range(6):
            ins = jnp.where(inside[q], 1.0, 0.0)
            differ = pnear[q] != pc
            flux = flux + ins * jnp.where(differ, -2.0 * c, near[q] - c)
            faces = faces + ins * jnp.where(differ, 1.0, 0.0)
            wts[q, rows, :] = ins * (0.5 * (beta + jnp.where(pnear[q] > 0, 1.0, 4.0)) - 1.0)
        heated = c + 0.06 * conduct * flux
        tnext_ref[z, pl.ds(pl.multiple_of(8 * i, 8), 8), :] = heated
        mass[rows, :] = 2.0 * conduct * faces * heated
        return carry

    lax.fori_loop(0, 64, head_chunk, 0)

    ra = lax.broadcasted_iota(jnp.int32, (128, 16), 0)
    ca = lax.broadcasted_iota(jnp.int32, (128, 16), 1)
    pick = jnp.where(ra % 16 == ca, 1.0, 0.0).astype(F32)
    rb = lax.broadcasted_iota(jnp.int32, (128, 128), 0)
    cb = lax.broadcasted_iota(jnp.int32, (128, 128), 1)
    hp = lax.Precision.HIGHEST
    spread = lax.dot_general(pick, north_ref[...], (((1,), (0,)), ((), ())), precision=hp, preferred_element_type=F32)
    spread = lax.dot_general(spread, pick, (((1,), (1,)), ((), ())), precision=hp, preferred_element_type=F32)
    north_all = jnp.where(rb // 16 == cb // 16, spread, 0.0)
    east = east_ref[...]
    for t in range(4):
        lanes = slice(t * 128, (t + 1) * 128)
        across = lax.dot_general(mass[:, lanes], east, (((1,), (1,)), ((), ())), precision=hp, preferred_element_type=F32)
        tile = (rb // 16) * 4 + t
        listed = jnp.zeros((128, 128), F32)
        for e in range(16):
            listed = jnp.where(tile == table_ref[e], 0.3, listed)
        for z in range(4):
            src = lax.dot_general(
                north_all, across[z * 128 : (z + 1) * 128], (((1,), (0,)), ((), ())), precision=hp, preferred_element_type=F32
            )
            f_ref[z * 128 : (z + 1) * 128, lanes] = listed * src
    for z in range(4):
        resid_ref[z] = f_ref[z * 128 : (z + 1) * 128, :]

    half = lax.broadcasted_iota(jnp.int32, (64, 8, 256), 1) < 4
    nn, nt = ((1,), (0,)), ((1,), (1,))

    def parts_of(ref, passes):
        return [ref[i] for i in range(3 if passes == 6 else 2)]

    def width(passes):
        return 3 if passes == 6 else 2

    def bulk(j, src_of, recv, ssem, rsem):
        def send(step, carry):
            pw, pn = peer(step, w, n)
            pltpu.make_async_remote_copy(
                src_ref=src_of(pn * NW + pw),
                dst_ref=recv.at[j, me],
                send_sem=ssem.at[j],
                recv_sem=rsem.at[j],
                device_id=(pw, pn),
                device_id_type=MESH,
            ).start()
            return carry

        lax.fori_loop(1, ND, send, 0)

    def gather(j, ag, ssem, rsem):
        def send(step, carry):
            pw, pn = peer(step, w, n)
            pltpu.make_async_remote_copy(
                src_ref=ag.at[j, me],
                dst_ref=ag.at[j, me],
                send_sem=ssem.at[j],
                recv_sem=rsem.at[j],
                device_id=(pw, pn),
                device_id_type=MESH,
            ).start()
            return carry

        lax.fori_loop(1, ND, send, 0)

    def wait_others(j, ref, sem):
        part = ref.at[j, pl.ds(0, ND - 1)]
        pltpu.make_async_copy(part, part, sem.at[j]).wait()

    def wait_all(j, ref, sem):
        part = ref.at[j]
        pltpu.make_async_copy(part, part, sem.at[j]).wait()

    def summed(rows):
        return jnp.sum(rows, axis=1, keepdims=True)

    def read_a(j):
        wait_others(j, ag_a, sem_ar)
        wait_others(j, ag_a, sem_as)
        return summed(jnp.sum(ag_a[j], axis=0))

    def one_pass(j, rho):
        first = j == 0
        table = parts_of(tx_ref, FWD)
        s_half = []
        for h in range(2):
            f = split(f_ref[h * 256 : (h + 1) * 256, :], width(FWD))
            s_half.append(product(table, f, nt, FWD).reshape(64, 8, 256))
        sbf[:, 0] = jnp.where(half, s_half[0], pltpu.roll(s_half[1], 4, 1))
        sbf[:, 1] = jnp.where(half, pltpu.roll(s_half[0], 4, 1), s_half[1])
        own = pltpu.make_async_copy(sbf.at[me // 2, me % 2], recvf.at[j, me], sem_fr.at[j])
        own.start()
        bulk(j, lambda p: sbf.at[p // 2, p % 2], recvf, sem_fs, sem_fr)
        gather(j, ag_a, sem_as, sem_ar)
        wait_all(j, recvf, sem_fr)
        table = parts_of(ty_ref, FWD)
        u = []
        for zl in range(2):
            a = jnp.concatenate(
                [
                    recvf[j, q * 32 : (q + 1) * 32, :, zl * 128 : (zl + 1) * 128].reshape(256, 128)
                    for q in range(NN)
                ],
                axis=1,
            )
            u.append(product(split(a, width(FWD)), table, nt, FWD))
        u = jnp.concatenate(u, axis=0)
        v = product(parts_of(b_ref, FWD), split(u, width(FWD)), nn, FWD)
        pi = read_a(j)
        alpha = jnp.where(first, -1.0, rho / pi)
        step = jnp.where(first, 0.0, rho / pi)
        left = c_ref[...] - alpha * v
        c_ref[...] = left
        scaled = left * inv_ref[...]
        q_part = jnp.sum(left * scaled, axis=0, keepdims=True)
        ag_b[j, me] = q_part[:, 0:128] + q_part[:, 128:256] + q_part[:, 256:384] + q_part[:, 384:512]
        back = product(parts_of(bt_ref, INV), split(scaled, width(INV)), nn, INV)
        table = parts_of(ty_ref, INV)
        for zl in range(2):
            r = product(split(back[zl * 256 : (zl + 1) * 256], width(INV)), table, nn, INV)
            for q in range(NN):
                sbi[q * 32 : (q + 1) * 32, :, zl * 128 : (zl + 1) * 128] = r[:, q * 128 : (q + 1) * 128].reshape(32, 8, 128)
        own = pltpu.make_async_copy(sbi.at[me], recvi.at[j, me], sem_ir.at[j])
        own.start()
        bulk(j, lambda p: sbi.at[p], recvi, sem_is, sem_ir)
        gather(j, ag_b, sem_bs, sem_br)
        wait_others(j, recvf, sem_fs)
        wait_all(j, recvi, sem_ir)
        wait_others(j, ag_b, sem_br)
        wait_others(j, ag_b, sem_bs)
        wait_others(j, recvi, sem_is)
        fresh = summed(jnp.sum(ag_b[j], axis=0))
        mix = jnp.where(first, 0.0, fresh / rho)
        got = recvi[j].reshape(64, 2, 8, 256)
        even, odd = got[:, 0], got[:, 1]
        halves = (
            jnp.where(half, even, pltpu.roll(odd, 4, 1)).reshape(ROWS, 256),
            jnp.where(half, pltpu.roll(even, 4, 1), odd).reshape(ROWS, 256),
        )
        table = parts_of(tx_ref, INV)
        for h in range(2):
            r = product(split(halves[h].T, width(INV)), table, nn, INV)
            spad[j, 1 + 2 * h : 3 + 2 * h, 8:136, :] = r.reshape(2, 128, NX)
        field = spad.at[j]
        copies = halo(2 + j, lambda z, y: field.at[(z + 1) if isinstance(z, int) else pl.ds(1, 4), y], 8, lambda z, y: field.at[z, y])
        for copy in copies:
            copy.start()

        def update(g, carry):
            z, i = g // 16, g % 16
            rows = pl.ds(pl.multiple_of(8 * g, 8), 8)
            line = pl.ds(pl.multiple_of(8 * i, 8), 8)
            d = d_ref[rows, :]
            press_ref[z, line, :] = press_ref[z, line, :] + step * d
            resid_ref[z, line, :] = resid_ref[z, line, :] - step * f_ref[rows, :]
            d_ref[rows, :] = spad[j, z + 1, pl.ds(pl.multiple_of(8 + 8 * i, 8), 8), :] + mix * d
            return carry

        lax.fori_loop(0, 64, update, 0)
        for copy in copies:
            copy.wait()

        def stencil(g, carry):
            z, i = g // 16, g % 16
            rows = pl.ds(pl.multiple_of(8 * g, 8), 8)
            c, near = around(field, z, i)
            total = resid_ref[z, pl.ds(pl.multiple_of(8 * i, 8), 8), :] + mix * f_ref[rows, :]
            for q in range(6):
                total = total + wts[q, rows, :] * (c - near[q])
            f_ref[rows, :] = total
            return carry + d_ref[rows, :] * total

        zero = jnp.zeros((8, NX), F32)
        line = jnp.sum(lax.fori_loop(0, 64, stencil, zero), axis=0, keepdims=True)
        ag_a[j + 1, me] = line[:, 0:128] + line[:, 128:256] + line[:, 256:384] + line[:, 384:512]
        return fresh

    rho = lax.fori_loop(0, ITERS, one_pass, jnp.ones((1, 1), F32))
    gather(ITERS, ag_a, sem_as, sem_ar)
    alpha = rho / read_a(ITERS)

    def finish(g, carry):
        z, i = g // 16, g % 16
        rows = pl.ds(pl.multiple_of(8 * g, 8), 8)
        line = pl.ds(pl.multiple_of(8 * i, 8), 8)
        press_ref[z, line, :] = press_ref[z, line, :] + alpha * d_ref[rows, :]
        resid_ref[z, line, :] = resid_ref[z, line, :] - alpha * f_ref[rows, :]
        return carry

    lax.fori_loop(0, 64, finish, 0)


def on_device(temp, phase, table, north, east):
    w = lax.axis_index("wide")
    n = lax.axis_index("narrow")
    me = n * NW + w
    ez = eigen_np(NZ)
    ex = eigen_np(NX).astype(np.float32)
    ey = eigen_np(NY).astype(np.float32)
    own = lax.dynamic_slice(jnp.asarray(ex), (4 * me,), (4,))
    rowden = (jnp.asarray((ez + 0.01).astype(np.float32))[:, None] + own[None, :]).reshape(ROWS, 1)
    colden = jnp.asarray(ey).reshape(1, NY)
    bz = z_table()
    tables = [jnp.asarray(split_np(t)) for t in (cosine_np(NX), cosine_np(NY), bz, bz.T)]
    vmem = pl.BlockSpec(memory_space=pltpu.VMEM)
    smem = pl.BlockSpec(memory_space=pltpu.SMEM)
    shape = jax.ShapeDtypeStruct((4, 128, NX), F32)
    dma = pltpu.SemaphoreType.DMA
    square = pltpu.VMEM((ROWS, NX), F32)
    return pl.pallas_call(
        whole_kernel,
        out_shape=(shape, shape, shape),
        in_specs=[vmem, vmem, smem] + [vmem] * 8,
        out_specs=(vmem, vmem, vmem),
        scratch_shapes=[
            pltpu.VMEM((6, 144, NX), F32),
            pltpu.VMEM((6, 144, NX), jnp.int32),
            pltpu.VMEM((ITERS, 6, 144, NX), F32),
            pltpu.VMEM((6, ROWS, NX), F32),
            square,
            square,
            square,
            square,
            square,
            pltpu.VMEM((64, 2, 8, 256), F32),
            pltpu.VMEM((ND, 8, 256), F32),
            pltpu.VMEM((ITERS, ND, 8, 256), F32),
            pltpu.VMEM((ITERS, ND, 8, 256), F32),
            pltpu.VMEM((ITERS + 1, ND, 1, 128), F32),
            pltpu.VMEM((ITERS, ND, 1, 128), F32),
            dma((ITERS,)),
            dma((ITERS,)),
            dma((ITERS,)),
            dma((ITERS,)),
            dma((ITERS + 1,)),
            dma((ITERS + 1,)),
            dma((ITERS,)),
            dma((ITERS,)),
            dma((5, 4)),
            dma((5, 4)),
        ],
        compiler_params=pltpu.CompilerParams(
            collective_id=0, has_side_effects=True, vmem_limit_bytes=60 * 2**20
        ),
    )(temp, phase, table.reshape(16), north, east, *tables, rowden, colden)


def solution(mesh):
    block = P("wide", "narrow", None)
    return jax.shard_map(
        on_device,
        mesh=mesh,
        in_specs=(block, block, block, P(), P()),
        out_specs=(block, block, block),
        check_vma=False,
    )
```

time: 535 us -> 207 us (0.39); the launches traced: 524 us -> 206 us
  blocking collectives: 281 us -> 0 us
  Pallas kernels: 0 us -> 199 us
  matrix products: 92.4 us -> 0 us
  starting transfers between devices: 49.2 us -> 0 us
  other arithmetic: 36.1 us -> 0.73 us
  waiting for transfers between devices: 34.3 us -> 0 us
  local copies, waits for them, and re-layouts: 22.7 us -> 5.94 us
  between operations: 8.12 us -> 0.67 us
    pallas_call x0 -> x1, Pallas kernels: none -> 199 us  [on_device(): pl.pallas_call(whole_kernel, out_shape=(shape, shape, shape), in_specs=[v...]
    psum x20 -> x0, blocking collectives: 164 us -> none  [over_axes(): array = lax.psum(array, axis)]
    all_to_all x5 -> x0, blocking collectives: 117 us -> none  [the longest x3 69 us: precondition(): lax.all_to_all(planes, WIDE_NARROW, split_axis=0, concat_axis=3, tiled=True)]
    dot_general x22 -> x0, matrix products: 92.4 us -> none  [the longest x3 21.7 us: precondition(): planes = jnp.einsum('mnyk,lny->mlk', planes, table_y, precision=highest)]
    ppermute x16 -> x0, starting transfers between devices: 30.1 us -> none  [the longest x8 19.8 us: padded_2(): lax.ppermute(last, axis, up)]
    all_to_all x1 -> x0, starting transfers between devices: 19.1 us -> none  [precondition(): lax.all_to_all(spectrum[None], WIDE_NARROW, split_axis=3, concat_axis=0,...]
    all_to_all x1 -> x0, waiting for transfers between devices: 18.6 us -> none  [precondition(): lax.all_to_all(spectrum[None], WIDE_NARROW, split_axis=3, concat_axis=0,...]
    ppermute x16 -> x0, waiting for transfers between devices: 15.7 us -> none  [the longest x8 15.6 us: padded_2(): lax.ppermute(initial, axis, [(b, a) for a, b in up])]
  transfers between devices with their start and end apart: 17 -> 0, of which waited for: 5 -> 0; matrix products, arithmetic and copies ran while one was open for 0% -> 0% of each run, Pallas kernels for 0% -> 0%
where the time goes in v1:
time: 207 us; the launch traced here: 206 us
  Pallas kernels  199 us (96%)
  local copies, waits for them, and re-layouts  5.94 us (3%)
    pallas_call x1, Pallas kernels, on_device(): pl.pallas_call(whole_kernel, out_shape=(shape, shape, shape), in_specs=[v...  199 us
    unnamed x7, local copies, waits for them, and re-layouts  4.36 us

profile of v1, /device:TPU:0, one launch (start us, length us, event | category | flops | bytes accessed | tf_op | source)
XLA Modules:
  0.0 206.0 jit_solution(6220393201961604957)
XLA Ops:
  0.6 0.8 dynamic_slice.3
  1.4 0.7 broadcast_add_fusion
  2.1 0.8 add.35.rowden_ref
  3.0 198.7 %shard_map.139 = (f32[4,128,512]{2,1,0:T(8,128)}, f32[4,128,512]{2,1,0:T(8,128)}, f32[4,128,512]{2,1,0:T(8,128)}) custom-call(f32[4,128,512]{2,1,0:T(8,128)} %temp_ref.1, s32[4,128,512]{2,1,0:T(8,128)} %phase_ref.1, s32[16]{0:T(128)} %bitcast.1, f32[16,16]{1,0:T(8,128)} %north_ref.1, f32[128,128]{1,0:T(8,128)} %east_ref.1, ...), custom_call_target="tpu_custom_call" | custom-call | tf_op jit(solution)/shard_map/pallas_call | solution.py:394
  201.6 0.0 copy-start.1
  201.6 0.0 copy-start
  201.6 2.4 %copy.19 = f32[4,128,512]{2,1,0:T(8,128)} copy(f32[4,128,512]{2,1,0:T(8,128)} %get-tuple-element.6) | data formatting | bytes 2097152
  204.0 0.0 copy-done.1
  204.1 1.0 copy.20
  205.0 0.0 copy-done
  205.0 1.0 copy.21
Async XLA Ops:
  201.6 2.4 %copy-start.1 = (f32[4,128,512]{2,1,0:T(8,128)S(1)}, f32[4,128,512]{2,1,0:T(8,128)}, u32[]{:S(2)}) copy-start(f32[4,128,512]{2,1,0:T(8,128)} %get-tuple-element.7) | copy-start | bytes 3145732
  201.6 3.4 %copy-start = (f32[4,128,512]{2,1,0:T(8,128)S(1)}, f32[4,128,512]{2,1,0:T(8,128)}, u32[]{:S(2)}) copy-start(f32[4,128,512]{2,1,0:T(8,128)} %get-tuple-element.8) | copy-start | bytes 3145732

commit v2 on v1

--- a/solution.py
+++ b/solution.py
@@ -18,7 +18,7 @@
 ND = NW * NN
 ITERS = 3
 ROWS = 512
-FWD, INV = 3, 3
+LINES = 17
 
 
 def cosine_np(m):
@@ -35,7 +35,7 @@
 def split_np(table):
     parts = []
     rest = table.astype(np.float64)
-    for _ in range(3):
+    for _ in range(2):
         part = rest.astype(np.float32).astype(ml_dtypes.bfloat16)
         parts.append(part)
         rest = rest - part.astype(np.float64)
@@ -50,22 +50,14 @@
     return big.reshape(ROWS, ROWS)
 
 
-def split(x, parts):
-    out = []
-    for i in range(parts):
-        part = x.astype(BF16)
-        out.append(part)
-        if i + 1 < parts:
-            x = x - part.astype(F32)
-    return out
-
-
-PAIRS = {3: ((0, 1), (1, 0), (0, 0)), 6: ((1, 1), (0, 2), (2, 0), (0, 1), (1, 0), (0, 0))}
-
-
-def product(a, b, dims, passes):
+def split(x):
+    high = x.astype(BF16)
+    return high, (x - high.astype(F32)).astype(BF16)
+
+
+def product(a, b, dims):
     total = None
-    for i, j in PAIRS[passes]:
+    for i, j in ((0, 1), (1, 0), (0, 0)):
         term = lax.dot_general(a[i], b[j], (dims, ((), ())), preferred_element_type=F32)
         total = term if total is None else total + term
     return total
@@ -78,11 +70,11 @@
 
 
 def whole_kernel(
-    temp_ref, phase_ref, table_ref, north_ref, east_ref, tx_ref, ty_ref, b_ref, bt_ref, rowden_ref, colden_ref,
+    temp_ref, phase_ref, table_ref, north_ref, east_ref, tx_ref, ty_ref, b_ref, bt_ref, ez_ref, ey_ref, ex_ref,
     tnext_ref, press_ref, resid_ref,
     tpad, ppad, spad, wts, mass, f_ref, c_ref, d_ref, inv_ref,
-    sbf, sbi, recvf, recvi, ag_a, ag_b,
-    sem_fs, sem_fr, sem_is, sem_ir, sem_as, sem_ar, sem_bs, sem_br, sem_hs, sem_hr,
+    sbf, sbi, recvf, recvi, red_n, red_w,
+    sem_fs, sem_fr, sem_is, sem_ir, sem_rs, sem_rr, sem_hs, sem_hr, sem_ready,
 ):
     w = lax.axis_index("wide")
     n = lax.axis_index("narrow")
@@ -90,22 +82,35 @@
 
     barrier = pltpu.get_barrier_semaphore()
 
-    def greet(step, carry):
-        pw, pn = peer(step, w, n)
-        pl.semaphore_signal(barrier, inc=1, device_id=(pw, pn), device_id_type=MESH)
+    def greet_narrow(step, carry):
+        pl.semaphore_signal(barrier, inc=1, device_id=(w, (n + step) % NN), device_id_type=MESH)
         return carry
 
-    lax.fori_loop(1, ND, greet, 0)
+    def greet_wide(step, carry):
+        pl.semaphore_signal(barrier, inc=1, device_id=((w + step) % NW, n), device_id_type=MESH)
+        return carry
+
+    lax.fori_loop(1, NN, greet_narrow, 0)
+    lax.fori_loop(1, NW, greet_wide, 0)
 
     tpad[1:5, 8:136, :] = temp_ref[...]
     ppad[1:5, 8:136, :] = phase_ref[...]
-    inv_ref[...] = 1.0 / (rowden_ref[...] + colden_ref[...])
+    lane = lax.broadcasted_iota(jnp.int32, (8, NX), 1)
+    own_k = lax.broadcasted_iota(jnp.int32, (8, NX), 0) % 4 + 4 * me
+    ex = jnp.sum(jnp.where(lane == own_k, ex_ref[...], 0.0), axis=1, keepdims=True)
+    den = ez_ref[...] + ex[None] + ey_ref[...][None]
+    inv_ref[...] = (1.0 / den).reshape(ROWS, NX)
     c_ref[...] = jnp.zeros_like(c_ref)
     d_ref[...] = jnp.zeros_like(d_ref)
     press_ref[...] = jnp.zeros_like(press_ref)
-    ag_a[0, me] = jnp.ones((1, 128), F32)
-
-    pl.semaphore_wait(barrier, ND - 1)
+
+    pl.semaphore_wait(barrier, NN - 1 + NW - 1)
+
+    def relay(step, carry):
+        pl.semaphore_signal(sem_ready, inc=1, device_id=(w, (n + step) % NN), device_id_type=MESH)
+        return carry
+
+    lax.fori_loop(1, NN, relay, 0)
 
     w_up, w_down = (w + 1) % NW, (w + NW - 1) % NW
     n_up, n_down = (n + 1) % NN, (n + NN - 1) % NN
@@ -181,7 +186,8 @@
         mass[rows, :] = 2.0 * conduct * faces * heated
         return carry
 
-    lax.fori_loop(0, 64, head_chunk, 0)
+    lax.fori_loop(0, 64, head_chunk, 0, unroll=2)
+    pl.semaphore_wait(sem_ready, NN - 1)
 
     ra = lax.broadcasted_iota(jnp.int32, (128, 16), 0)
     ca = lax.broadcasted_iota(jnp.int32, (128, 16), 1)
@@ -208,21 +214,18 @@
     for z in range(4):
         resid_ref[z] = f_ref[z * 128 : (z + 1) * 128, :]
 
-    half = lax.broadcasted_iota(jnp.int32, (64, 8, 256), 1) < 4
+    half = lax.broadcasted_iota(jnp.int32, (64, 8, 128), 1) < 4
     nn, nt = ((1,), (0,)), ((1,), (1,))
 
-    def parts_of(ref, passes):
-        return [ref[i] for i in range(3 if passes == 6 else 2)]
-
-    def width(passes):
-        return 3 if passes == 6 else 2
+    def parts_of(ref):
+        return ref[0], ref[1]
 
     def bulk(j, src_of, recv, ssem, rsem):
         def send(step, carry):
             pw, pn = peer(step, w, n)
             pltpu.make_async_remote_copy(
                 src_ref=src_of(pn * NW + pw),
-                dst_ref=recv.at[j, me],
+                dst_ref=recv.at[j, me, pl.ds(0, LINES)],
                 send_sem=ssem.at[j],
                 recv_sem=rsem.at[j],
                 device_id=(pw, pn),
@@ -232,98 +235,81 @@
 
         lax.fori_loop(1, ND, send, 0)
 
-    def gather(j, ag, ssem, rsem):
-        def send(step, carry):
-            pw, pn = peer(step, w, n)
-            pltpu.make_async_remote_copy(
-                src_ref=ag.at[j, me],
-                dst_ref=ag.at[j, me],
-                send_sem=ssem.at[j],
-                recv_sem=rsem.at[j],
-                device_id=(pw, pn),
-                device_id_type=MESH,
-            ).start()
-            return carry
-
-        lax.fori_loop(1, ND, send, 0)
-
     def wait_others(j, ref, sem):
-        part = ref.at[j, pl.ds(0, ND - 1)]
+        part = ref.at[j, pl.ds(0, ND - 1), pl.ds(0, LINES)]
         pltpu.make_async_copy(part, part, sem.at[j]).wait()
 
     def wait_all(j, ref, sem):
-        part = ref.at[j]
+        part = ref.at[j, :, pl.ds(0, LINES)]
         pltpu.make_async_copy(part, part, sem.at[j]).wait()
+
+    def folded(line):
+        return line[:, 0:128] + line[:, 128:256] + line[:, 256:384] + line[:, 384:512]
 
     def summed(rows):
         return jnp.sum(rows, axis=1, keepdims=True)
 
-    def read_a(j):
-        wait_others(j, ag_a, sem_ar)
-        wait_others(j, ag_a, sem_as)
-        return summed(jnp.sum(ag_a[j], axis=0))
-
-    def one_pass(j, rho):
+    def one_pass(j, carry):
+        rho, line = carry
         first = j == 0
-        table = parts_of(tx_ref, FWD)
-        s_half = []
-        for h in range(2):
-            f = split(f_ref[h * 256 : (h + 1) * 256, :], width(FWD))
-            s_half.append(product(table, f, nt, FWD).reshape(64, 8, 256))
-        sbf[:, 0] = jnp.where(half, s_half[0], pltpu.roll(s_half[1], 4, 1))
-        sbf[:, 1] = jnp.where(half, pltpu.roll(s_half[0], 4, 1), s_half[1])
-        own = pltpu.make_async_copy(sbf.at[me // 2, me % 2], recvf.at[j, me], sem_fr.at[j])
+        table = parts_of(tx_ref)
+        low = product(table, split(f_ref[0:256, :]), nt)
+        high = product(table, split(f_ref[256:512, :]), nt)
+        for zl in range(2):
+            a = low[:, zl * 128 : (zl + 1) * 128].reshape(64, 8, 128)
+            b = high[:, zl * 128 : (zl + 1) * 128].reshape(64, 8, 128)
+            sbf[:, 0, zl * 8 : (zl + 1) * 8, :] = jnp.where(half, a, pltpu.roll(b, 4, 1))
+            sbf[:, 1, zl * 8 : (zl + 1) * 8, :] = jnp.where(half, pltpu.roll(a, 4, 1), b)
+        sbf[:, :, 16:17, :] = jnp.broadcast_to(line, (64, 2, 1, 128))
+        sent = pl.ds(0, LINES)
+        own = pltpu.make_async_copy(sbf.at[me // 2, me % 2, sent], recvf.at[j, me, sent], sem_fr.at[j])
         own.start()
-        bulk(j, lambda p: sbf.at[p // 2, p % 2], recvf, sem_fs, sem_fr)
-        gather(j, ag_a, sem_as, sem_ar)
+        bulk(j, lambda p: sbf.at[p // 2, p % 2, sent], recvf, sem_fs, sem_fr)
         wait_all(j, recvf, sem_fr)
-        table = parts_of(ty_ref, FWD)
+        table = parts_of(ty_ref)
         u = []
         for zl in range(2):
             a = jnp.concatenate(
                 [
-                    recvf[j, q * 32 : (q + 1) * 32, :, zl * 128 : (zl + 1) * 128].reshape(256, 128)
+                    recvf[j, q * 32 : (q + 1) * 32, zl * 8 : (zl + 1) * 8, :].reshape(256, 128)
                     for q in range(NN)
                 ],
                 axis=1,
             )
-            u.append(product(split(a, width(FWD)), table, nt, FWD))
+            u.append(product(split(a), table, nt))
         u = jnp.concatenate(u, axis=0)
-        v = product(parts_of(b_ref, FWD), split(u, width(FWD)), nn, FWD)
-        pi = read_a(j)
+        v = product(parts_of(b_ref), split(u), nn)
+        pi = summed(jnp.sum(recvf[j, :, 16:17, :], axis=0))
         alpha = jnp.where(first, -1.0, rho / pi)
         step = jnp.where(first, 0.0, rho / pi)
         left = c_ref[...] - alpha * v
         c_ref[...] = left
         scaled = left * inv_ref[...]
         q_part = jnp.sum(left * scaled, axis=0, keepdims=True)
-        ag_b[j, me] = q_part[:, 0:128] + q_part[:, 128:256] + q_part[:, 256:384] + q_part[:, 384:512]
-        back = product(parts_of(bt_ref, INV), split(scaled, width(INV)), nn, INV)
-        table = parts_of(ty_ref, INV)
+        sbi[:, 16:17, :] = jnp.broadcast_to(folded(q_part), (ND, 1, 128))
+        back = product(parts_of(bt_ref), split(scaled), nn)
+        table = parts_of(ty_ref)
         for zl in range(2):
-            r = product(split(back[zl * 256 : (zl + 1) * 256], width(INV)), table, nn, INV)
+            r = product(split(back[zl * 256 : (zl + 1) * 256]), table, nn)
             for q in range(NN):
-                sbi[q * 32 : (q + 1) * 32, :, zl * 128 : (zl + 1) * 128] = r[:, q * 128 : (q + 1) * 128].reshape(32, 8, 128)
-        own = pltpu.make_async_copy(sbi.at[me], recvi.at[j, me], sem_ir.at[j])
+                sbi[q * 32 : (q + 1) * 32, zl * 8 : (zl + 1) * 8, :] = r[:, q * 128 : (q + 1) * 128].reshape(32, 8, 128)
+        own = pltpu.make_async_copy(sbi.at[me, sent], recvi.at[j, me, sent], sem_ir.at[j])
         own.start()
-        bulk(j, lambda p: sbi.at[p], recvi, sem_is, sem_ir)
-        gather(j, ag_b, sem_bs, sem_br)
+        bulk(j, lambda p: sbi.at[p, sent], recvi, sem_is, sem_ir)
         wait_others(j, recvf, sem_fs)
         wait_all(j, recvi, sem_ir)
-        wait_others(j, ag_b, sem_br)
-        wait_others(j, ag_b, sem_bs)
         wait_others(j, recvi, sem_is)
-        fresh = summed(jnp.sum(ag_b[j], axis=0))
+        fresh = summed(jnp.sum(recvi[j, :, 16:17, :], axis=0))
         mix = jnp.where(first, 0.0, fresh / rho)
-        got = recvi[j].reshape(64, 2, 8, 256)
-        even, odd = got[:, 0], got[:, 1]
-        halves = (
-            jnp.where(half, even, pltpu.roll(odd, 4, 1)).reshape(ROWS, 256),
-            jnp.where(half, pltpu.roll(even, 4, 1), odd).reshape(ROWS, 256),
-        )
-        table = parts_of(tx_ref, INV)
+        planes = [[], []]
+        for zl in range(2):
+            got = recvi[j, :, zl * 8 : (zl + 1) * 8, :].reshape(64, 2, 8, 128)
+            even, odd = got[:, 0], got[:, 1]
+            planes[0].append(jnp.where(half, even, pltpu.roll(odd, 4, 1)).reshape(ROWS, 128).T)
+            planes[1].append(jnp.where(half, pltpu.roll(even, 4, 1), odd).reshape(ROWS, 128).T)
+        table = parts_of(tx_ref)
         for h in range(2):
-            r = product(split(halves[h].T, width(INV)), table, nn, INV)
+            r = product(split(jnp.concatenate(planes[h], axis=0)), table, nn)
             spad[j, 1 + 2 * h : 3 + 2 * h, 8:136, :] = r.reshape(2, 128, NX)
         field = spad.at[j]
         copies = halo(2 + j, lambda z, y: field.at[(z + 1) if isinstance(z, int) else pl.ds(1, 4), y], 8, lambda z, y: field.at[z, y])
@@ -340,7 +326,7 @@
             d_ref[rows, :] = spad[j, z + 1, pl.ds(pl.multiple_of(8 + 8 * i, 8), 8), :] + mix * d
             return carry
 
-        lax.fori_loop(0, 64, update, 0)
+        lax.fori_loop(0, 64, update, 0, unroll=4)
         for copy in copies:
             copy.wait()
 
@@ -355,13 +341,33 @@
             return carry + d_ref[rows, :] * total
 
         zero = jnp.zeros((8, NX), F32)
-        line = jnp.sum(lax.fori_loop(0, 64, stencil, zero), axis=0, keepdims=True)
-        ag_a[j + 1, me] = line[:, 0:128] + line[:, 128:256] + line[:, 256:384] + line[:, 384:512]
-        return fresh
-
-    rho = lax.fori_loop(0, ITERS, one_pass, jnp.ones((1, 1), F32))
-    gather(ITERS, ag_a, sem_as, sem_ar)
-    alpha = rho / read_a(ITERS)
+        line = jnp.sum(lax.fori_loop(0, 64, stencil, zero, unroll=2), axis=0, keepdims=True)
+        return fresh, folded(line)
+
+    rho, line = lax.fori_loop(0, ITERS, one_pass, (jnp.ones((1, 1), F32), jnp.ones((1, 128), F32)))
+
+    def gather(slots, slot, count, to, ssem, rsem):
+        def send(step, carry):
+            pltpu.make_async_remote_copy(
+                src_ref=slots.at[slot],
+                dst_ref=slots.at[slot],
+                send_sem=ssem,
+                recv_sem=rsem,
+                device_id=to(step),
+                device_id_type=MESH,
+            ).start()
+            return carry
+
+        lax.fori_loop(1, count, send, 0)
+        part = slots.at[pl.ds(0, count - 1)]
+        pltpu.make_async_copy(part, part, rsem).wait()
+        pltpu.make_async_copy(part, part, ssem).wait()
+        return jnp.sum(slots[...], axis=0)
+
+    red_n[n] = line
+    red_w[w] = gather(red_n, n, NN, lambda step: (w, (n + step) % NN), sem_rs.at[0], sem_rr.at[0])
+    pi = summed(gather(red_w, w, NW, lambda step: ((w + step) % NW, n), sem_rs.at[1], sem_rr.at[1]))
+    alpha = rho / pi
 
     def finish(g, carry):
         z, i = g // 16, g % 16
@@ -371,19 +377,13 @@
         resid_ref[z, line, :] = resid_ref[z, line, :] - alpha * f_ref[rows, :]
         return carry
 
-    lax.fori_loop(0, 64, finish, 0)
+    lax.fori_loop(0, 64, finish, 0, unroll=4)
 
 
 def on_device(temp, phase, table, north, east):
-    w = lax.axis_index("wide")
-    n = lax.axis_index("narrow")
-    me = n * NW + w
-    ez = eigen_np(NZ)
-    ex = eigen_np(NX).astype(np.float32)
-    ey = eigen_np(NY).astype(np.float32)
-    own = lax.dynamic_slice(jnp.asarray(ex), (4 * me,), (4,))
-    rowden = (jnp.asarray((ez + 0.01).astype(np.float32))[:, None] + own[None, :]).reshape(ROWS, 1)
-    colden = jnp.asarray(ey).reshape(1, NY)
+    ez = np.repeat(eigen_np(NZ) + 0.01, 4).reshape(64, 8, 1).astype(np.float32)
+    ey = eigen_np(NY).astype(np.float32).reshape(1, NY)
+    ex = eigen_np(NX).astype(np.float32).reshape(1, NX)
     bz = z_table()
     tables = [jnp.asarray(split_np(t)) for t in (cosine_np(NX), cosine_np(NY), bz, bz.T)]
     vmem = pl.BlockSpec(memory_space=pltpu.VMEM)
@@ -394,7 +394,7 @@
     return pl.pallas_call(
         whole_kernel,
         out_shape=(shape, shape, shape),
-        in_specs=[vmem, vmem, smem] + [vmem] * 8,
+        in_specs=[vmem, vmem, smem] + [vmem] * 9,
         out_specs=(vmem, vmem, vmem),
         scratch_shapes=[
             pltpu.VMEM((6, 144, NX), F32),
@@ -406,27 +406,26 @@
             square,
             square,
             square,
-            pltpu.VMEM((64, 2, 8, 256), F32),
-            pltpu.VMEM((ND, 8, 256), F32),
-            pltpu.VMEM((ITERS, ND, 8, 256), F32),
-            pltpu.VMEM((ITERS, ND, 8, 256), F32),
-            pltpu.VMEM((ITERS + 1, ND, 1, 128), F32),
-            pltpu.VMEM((ITERS, ND, 1, 128), F32),
+            pltpu.VMEM((64, 2, 24, 128), F32),
+            pltpu.VMEM((ND, 24, 128), F32),
+            pltpu.VMEM((ITERS, ND, 24, 128), F32),
+            pltpu.VMEM((ITERS, ND, 24, 128), F32),
+            pltpu.VMEM((NN, 1, 128), F32),
+            pltpu.VMEM((NW, 1, 128), F32),
             dma((ITERS,)),
             dma((ITERS,)),
             dma((ITERS,)),
             dma((ITERS,)),
-            dma((ITERS + 1,)),
-            dma((ITERS + 1,)),
-            dma((ITERS,)),
-            dma((ITERS,)),
+            dma((2,)),
+            dma((2,)),
             dma((5, 4)),
             dma((5, 4)),
+            pltpu.SemaphoreType.REGULAR,
         ],
         compiler_params=pltpu.CompilerParams(
             collective_id=0, has_side_effects=True, vmem_limit_bytes=60 * 2**20
         ),
-    )(temp, phase, table.reshape(16), north, east, *tables, rowden, colden)
+    )(temp, phase, table.reshape(16), north, east, *tables, jnp.asarray(ez), jnp.asarray(ey), jnp.asarray(ex))
 
 
 def solution(mesh):

time: 207 us -> 186 us (0.90)
  Pallas kernels: 199 us -> 180 us
    pallas_call x1, Pallas kernels: 199 us -> 180 us  [on_device(): pl.pallas_call(whole_kernel, out_shape=(shape, shape, shape), in_specs=[v...]
where the time goes in v2:
time: 186 us; the launch traced here: 185 us
  Pallas kernels  180 us (97%)
  local copies, waits for them, and re-layouts  4.93 us (3%)
    pallas_call x1, Pallas kernels, on_device(): pl.pallas_call(whole_kernel, out_shape=(shape, shape, shape), in_specs=[v...  180 us
    unnamed x7, local copies, waits for them, and re-layouts  4.93 us

profile of v2, /device:TPU:0, one launch (start us, length us, event | category | flops | bytes accessed | tf_op | source)
XLA Modules:
  0.0 185.5 jit_solution(12493790503360254159)
XLA Ops:
  0.6 179.9 %shard_map.139 = (f32[4,128,512]{2,1,0:T(8,128)}, f32[4,128,512]{2,1,0:T(8,128)}, f32[4,128,512]{2,1,0:T(8,128)}) custom-call(f32[4,128,512]{2,1,0:T(8,128)} %temp_ref.1, s32[4,128,512]{2,1,0:T(8,128)} %phase_ref.1, s32[16]{0:T(128)} %bitcast.1, f32[16,16]{1,0:T(8,128)} %north_ref.1, f32[128,128]{1,0:T(8,128)} %east_ref.1, ...), custom_call_target="tpu_custom_call" | custom-call | tf_op jit(solution)/shard_map/pallas_call | solution.py:394
  180.5 0.0 copy-start.1
  180.5 2.4 %copy.18 = f32[4,128,512]{2,1,0:T(8,128)} copy(f32[4,128,512]{2,1,0:T(8,128)} %get-tuple-element.6) | data formatting | bytes 2097152
  182.9 0.0 copy-done.1
  182.9 0.0 copy-start
  182.9 1.0 copy.19
  183.9 0.6 copy-done
  184.5 1.0 copy.20
Async XLA Ops:
  180.5 2.4 %copy-start.1 = (f32[4,128,512]{2,1,0:T(8,128)S(1)}, f32[4,128,512]{2,1,0:T(8,128)}, u32[]{:S(2)}) copy-start(f32[4,128,512]{2,1,0:T(8,128)} %get-tuple-element.7) | copy-start | bytes 3145732
  182.9 1.6 copy-start

commit v3 on v2

--- a/solution.py
+++ b/solution.py
@@ -63,24 +63,57 @@
     return total
 
 
-def peer(step, w, n):
-    dx, dy, dz, dc = step % 4, (step // 4) % 4, (step // 16) % 4, step // 64
+HOPS = sorted(np.ndindex(3, 3, 3), key=lambda hops: -sum(hops))
+
+
+def each_peer(w, n, send):
     y, z, c = w // 8, (w // 2) % 4, w % 2
-    return ((y + dy) % 4) * 8 + ((z + dz) % 4) * 2 + (c + dc) % 2, (n + dx) % 4
+    for hops in HOPS:
+        ones = sum(h == 1 for h in hops)
+
+        def body(turn, carry, hops=hops):
+            flip, rest = turn % 2, turn // 2
+            offset = []
+            for h in hops:
+                if h == 1:
+                    offset.append(1 + 2 * (rest % 2))
+                    rest = rest // 2
+                else:
+                    offset.append(h)
+            dx, dy, dz = offset
+            send(((y + dy) % 4) * 8 + ((z + dz) % 4) * 2 + (c + flip) % 2, (n + dx) % 4)
+            return carry
+
+        lax.fori_loop(1 if sum(hops) == 0 else 0, 2 ** (ones + 1), body, 0)
 
 
 def whole_kernel(
-    temp_ref, phase_ref, table_ref, north_ref, east_ref, tx_ref, ty_ref, b_ref, bt_ref, ez_ref, ey_ref, ex_ref,
+    temp_ref, phase_ref, table_ref, north_ref, east_ref, tx_any, ty_any, b_any, bt_any, ez_ref, ey_ref, ex_ref,
     tnext_ref, press_ref, resid_ref,
-    tpad, ppad, spad, wts, mass, f_ref, c_ref, d_ref, inv_ref,
+    tx_ref, ty_ref, b_ref, bt_ref, tpad, ppad, spad, wts, mass, f_ref, c_ref, d_ref, inv_ref,
     sbf, sbi, recvf, recvi, red_n, red_w,
-    sem_fs, sem_fr, sem_is, sem_ir, sem_rs, sem_rr, sem_hs, sem_hr, sem_ready,
+    sem_fs, sem_fr, sem_is, sem_ir, sem_rs, sem_rr, sem_hs, sem_hr, sem_ready, sem_load,
 ):
     w = lax.axis_index("wide")
     n = lax.axis_index("narrow")
     me = n * NW + w
 
     barrier = pltpu.get_barrier_semaphore()
+    loads = [
+        pltpu.make_async_copy(a, b, sem_load.at[i])
+        for i, (a, b) in enumerate(
+            (
+                (temp_ref, tpad.at[pl.ds(1, 4), pl.ds(8, 128)]),
+                (phase_ref, ppad.at[pl.ds(1, 4), pl.ds(8, 128)]),
+                (tx_any, tx_ref),
+                (ty_any, ty_ref),
+                (b_any, b_ref),
+                (bt_any, bt_ref),
+            )
+        )
+    ]
+    for load in loads:
+        load.start()
 
     def greet_narrow(step, carry):
         pl.semaphore_signal(barrier, inc=1, device_id=(w, (n + step) % NN), device_id_type=MESH)
@@ -92,17 +125,6 @@
 
     lax.fori_loop(1, NN, greet_narrow, 0)
     lax.fori_loop(1, NW, greet_wide, 0)
-
-    tpad[1:5, 8:136, :] = temp_ref[...]
-    ppad[1:5, 8:136, :] = phase_ref[...]
-    lane = lax.broadcasted_iota(jnp.int32, (8, NX), 1)
-    own_k = lax.broadcasted_iota(jnp.int32, (8, NX), 0) % 4 + 4 * me
-    ex = jnp.sum(jnp.where(lane == own_k, ex_ref[...], 0.0), axis=1, keepdims=True)
-    den = ez_ref[...] + ex[None] + ey_ref[...][None]
-    inv_ref[...] = (1.0 / den).reshape(ROWS, NX)
-    c_ref[...] = jnp.zeros_like(c_ref)
-    d_ref[...] = jnp.zeros_like(d_ref)
-    press_ref[...] = jnp.zeros_like(press_ref)
 
     pl.semaphore_wait(barrier, NN - 1 + NW - 1)
 
@@ -140,8 +162,16 @@
     head += halo(1, lambda z, y: phase_ref.at[z, y], 0, lambda z, y: ppad.at[z, y])
     for copy in head:
         copy.start()
-    for copy in head:
-        copy.wait()
+    lane = lax.broadcasted_iota(jnp.int32, (8, NX), 1)
+    own_k = lax.broadcasted_iota(jnp.int32, (8, NX), 0) % 4 + 4 * me
+    ex = jnp.sum(jnp.where(lane == own_k, ex_ref[...], 0.0), axis=1, keepdims=True)
+    den = ez_ref[...] + ex[None] + ey_ref[...][None]
+    inv_ref[...] = (1.0 / den).reshape(ROWS, NX)
+    c_ref[...] = jnp.zeros_like(c_ref)
+    d_ref[...] = jnp.zeros_like(d_ref)
+    press_ref[...] = jnp.zeros_like(press_ref)
+    for load in loads:
+        load.wait()
 
     row8 = lax.broadcasted_iota(jnp.int32, (8, NX), 0)
     lane8 = lax.broadcasted_iota(jnp.int32, (8, NX), 1)
@@ -163,9 +193,25 @@
         )
         return c, near
 
-    def head_chunk(g, carry):
-        z, i = g // 16, g % 16
-        rows = pl.ds(pl.multiple_of(8 * g, 8), 8)
+    def sweep(copies, body, carry):
+        carry = lax.fori_loop(0, 28, lambda q, c: body(1 + q // 14, 1 + q % 14, c), carry, unroll=2)
+        copies[2].wait()
+        copies[3].wait()
+        carry = lax.fori_loop(0, 4, lambda q, c: body(1 + q // 2, 15 * (q % 2), c), carry)
+        copies[0].wait()
+        copies[1].wait()
+        return lax.fori_loop(0, 32, lambda q, c: body(3 * (q // 16), q % 16, c), carry, unroll=2)
+
+    class Both:
+        def __init__(self, a, b):
+            self.pair = (a, b)
+
+        def wait(self):
+            for copy in self.pair:
+                copy.wait()
+
+    def head_chunk(z, i, carry):
+        rows = pl.ds(pl.multiple_of(8 * (16 * z + i), 8), 8)
         c, near = around(tpad, z, i)
         pc, pnear = around(ppad, z, i)
         gz = jnp.zeros_like(row8) + (4 * w + z)
@@ -186,7 +232,7 @@
         mass[rows, :] = 2.0 * conduct * faces * heated
         return carry
 
-    lax.fori_loop(0, 64, head_chunk, 0, unroll=2)
+    sweep([Both(head[i], head[4 + i]) for i in range(4)], head_chunk, 0)
     pl.semaphore_wait(sem_ready, NN - 1)
 
     ra = lax.broadcasted_iota(jnp.int32, (128, 16), 0)
@@ -221,8 +267,7 @@
         return ref[0], ref[1]
 
     def bulk(j, src_of, recv, ssem, rsem):
-        def send(step, carry):
-            pw, pn = peer(step, w, n)
+        def send(pw, pn):
             pltpu.make_async_remote_copy(
                 src_ref=src_of(pn * NW + pw),
                 dst_ref=recv.at[j, me, pl.ds(0, LINES)],
@@ -231,9 +276,8 @@
                 device_id=(pw, pn),
                 device_id_type=MESH,
             ).start()
-            return carry
-
-        lax.fori_loop(1, ND, send, 0)
+
+        each_peer(w, n, send)
 
     def wait_others(j, ref, sem):
         part = ref.at[j, pl.ds(0, ND - 1), pl.ds(0, LINES)]
@@ -296,6 +340,16 @@
         own = pltpu.make_async_copy(sbi.at[me, sent], recvi.at[j, me, sent], sem_ir.at[j])
         own.start()
         bulk(j, lambda p: sbi.at[p, sent], recvi, sem_is, sem_ir)
+
+        def update(g, carry):
+            z, i = g // 16, g % 16
+            rows = pl.ds(pl.multiple_of(8 * g, 8), 8)
+            line = pl.ds(pl.multiple_of(8 * i, 8), 8)
+            press_ref[z, line, :] = press_ref[z, line, :] + step * d_ref[rows, :]
+            resid_ref[z, line, :] = resid_ref[z, line, :] - step * f_ref[rows, :]
+            return carry
+
+        lax.fori_loop(0, 64, update, 0, unroll=4)
         wait_others(j, recvf, sem_fs)
         wait_all(j, recvi, sem_ir)
         wait_others(j, recvi, sem_is)
@@ -308,40 +362,29 @@
             planes[0].append(jnp.where(half, even, pltpu.roll(odd, 4, 1)).reshape(ROWS, 128).T)
             planes[1].append(jnp.where(half, pltpu.roll(even, 4, 1), odd).reshape(ROWS, 128).T)
         table = parts_of(tx_ref)
+        field = spad.at[j]
+        copies = halo(2 + j, lambda z, y: field.at[(z + 1) if isinstance(z, int) else pl.ds(1, 4), y], 8, lambda z, y: field.at[z, y])
         for h in range(2):
             r = product(split(jnp.concatenate(planes[h], axis=0)), table, nn)
             spad[j, 1 + 2 * h : 3 + 2 * h, 8:136, :] = r.reshape(2, 128, NX)
-        field = spad.at[j]
-        copies = halo(2 + j, lambda z, y: field.at[(z + 1) if isinstance(z, int) else pl.ds(1, 4), y], 8, lambda z, y: field.at[z, y])
-        for copy in copies:
-            copy.start()
-
-        def update(g, carry):
-            z, i = g // 16, g % 16
-            rows = pl.ds(pl.multiple_of(8 * g, 8), 8)
-            line = pl.ds(pl.multiple_of(8 * i, 8), 8)
-            d = d_ref[rows, :]
-            press_ref[z, line, :] = press_ref[z, line, :] + step * d
-            resid_ref[z, line, :] = resid_ref[z, line, :] - step * f_ref[rows, :]
-            d_ref[rows, :] = spad[j, z + 1, pl.ds(pl.multiple_of(8 + 8 * i, 8), 8), :] + mix * d
-            return carry
-
-        lax.fori_loop(0, 64, update, 0, unroll=4)
-        for copy in copies:
-            copy.wait()
-
-        def stencil(g, carry):
-            z, i = g // 16, g % 16
-            rows = pl.ds(pl.multiple_of(8 * g, 8), 8)
+            if h == 0:
+                copies[1].start()
+        copies[0].start()
+        copies[2].start()
+        copies[3].start()
+
+        def stencil(z, i, carry):
+            rows = pl.ds(pl.multiple_of(8 * (16 * z + i), 8), 8)
             c, near = around(field, z, i)
             total = resid_ref[z, pl.ds(pl.multiple_of(8 * i, 8), 8), :] + mix * f_ref[rows, :]
             for q in range(6):
                 total = total + wts[q, rows, :] * (c - near[q])
             f_ref[rows, :] = total
-            return carry + d_ref[rows, :] * total
-
-        zero = jnp.zeros((8, NX), F32)
-        line = jnp.sum(lax.fori_loop(0, 64, stencil, zero, unroll=2), axis=0, keepdims=True)
+            d = c + mix * d_ref[rows, :]
+            d_ref[rows, :] = d
+            return carry + d * total
+
+        line = jnp.sum(sweep(copies, stencil, jnp.zeros((8, NX), F32)), axis=0, keepdims=True)
         return fresh, folded(line)
 
     rho, line = lax.fori_loop(0, ITERS, one_pass, (jnp.ones((1, 1), F32), jnp.ones((1, 128), F32)))
@@ -387,6 +430,8 @@
     bz = z_table()
     tables = [jnp.asarray(split_np(t)) for t in (cosine_np(NX), cosine_np(NY), bz, bz.T)]
     vmem = pl.BlockSpec(memory_space=pltpu.VMEM)
+    anywhere = pl.BlockSpec(memory_space=pl.ANY)
+    tabled = pltpu.VMEM((2, ROWS, ROWS), BF16)
     smem = pl.BlockSpec(memory_space=pltpu.SMEM)
     shape = jax.ShapeDtypeStruct((4, 128, NX), F32)
     dma = pltpu.SemaphoreType.DMA
@@ -394,9 +439,13 @@
     return pl.pallas_call(
         whole_kernel,
         out_shape=(shape, shape, shape),
-        in_specs=[vmem, vmem, smem] + [vmem] * 9,
+        in_specs=[anywhere, anywhere, smem, vmem, vmem] + [anywhere] * 4 + [vmem] * 3,
         out_specs=(vmem, vmem, vmem),
         scratch_shapes=[
+            tabled,
+            tabled,
+            tabled,
+            tabled,
             pltpu.VMEM((6, 144, NX), F32),
             pltpu.VMEM((6, 144, NX), jnp.int32),
             pltpu.VMEM((ITERS, 6, 144, NX), F32),
@@ -421,6 +470,7 @@
             dma((5, 4)),
             dma((5, 4)),
             pltpu.SemaphoreType.REGULAR,
+            dma((6,)),
         ],
         compiler_params=pltpu.CompilerParams(
             collective_id=0, has_side_effects=True, vmem_limit_bytes=60 * 2**20

time: 186 us -> 173 us (0.930)
  Pallas kernels: 180 us -> 166 us
    pallas_call x1, Pallas kernels: 180 us -> 166 us  [on_device(): pl.pallas_call(whole_kernel, out_shape=(shape, shape, shape), in_specs=[a...]
where the time goes in v3:
time: 173 us; the launch traced here: 172 us
  Pallas kernels  166 us (96%)
  local copies, waits for them, and re-layouts  4.93 us (3%)
    pallas_call x1, Pallas kernels, on_device(): pl.pallas_call(whole_kernel, out_shape=(shape, shape, shape), in_specs=[a...  166 us
    unnamed x7, local copies, waits for them, and re-layouts  4.93 us

profile of v3, /device:TPU:0, one launch (start us, length us, event | category | flops | bytes accessed | tf_op | source)
XLA Modules:
  0.0 171.8 jit_solution(2333123024783981082)
XLA Ops:
  0.6 166.3 %shard_map.139 = (f32[4,128,512]{2,1,0:T(8,128)}, f32[4,128,512]{2,1,0:T(8,128)}, f32[4,128,512]{2,1,0:T(8,128)}) custom-call(f32[4,128,512]{2,1,0:T(8,128)} %temp_ref.1, s32[4,128,512]{2,1,0:T(8,128)} %phase_ref.1, s32[16]{0:T(128)} %bitcast.1, f32[16,16]{1,0:T(8,128)} %north_ref.1, f32[128,128]{1,0:T(8,128)} %east_ref.1, ...), custom_call_target="tpu_custom_call" | custom-call | tf_op jit(solution)/shard_map/pallas_call | solution.py:439
  166.9 0.0 copy-start.1
  166.9 2.4 %copy.18 = f32[4,128,512]{2,1,0:T(8,128)} copy(f32[4,128,512]{2,1,0:T(8,128)} %get-tuple-element.6) | data formatting | bytes 2097152
  169.3 0.0 copy-done.1
  169.3 0.0 copy-start
  169.3 1.0 copy.19
  170.2 0.6 copy-done
  170.9 1.0 copy.20
Async XLA Ops:
  166.9 2.4 %copy-start.1 = (f32[4,128,512]{2,1,0:T(8,128)S(1)}, f32[4,128,512]{2,1,0:T(8,128)}, u32[]{:S(2)}) copy-start(f32[4,128,512]{2,1,0:T(8,128)} %get-tuple-element.7) | copy-start | bytes 3145732
  169.3 1.6 copy-start

commit v4 on v3

--- a/solution.py
+++ b/solution.py
@@ -43,11 +43,11 @@
 
 
 def z_table():
-    table = cosine_np(NZ).reshape(NZ, NW, 2, 2).transpose(0, 3, 1, 2)
-    big = np.zeros((NZ, 4, 2, NW, 2, 4))
+    table = cosine_np(NZ)[:, 0::2].reshape(NZ // 2, 2, NZ // 2)
+    big = np.zeros((2, NZ // 2, 4, NZ // 2, 4))
     for k in range(4):
-        big[:, k, :, :, :, k] = table
-    return big.reshape(ROWS, ROWS)
+        big[:, :, k, :, k] = table.transpose(1, 0, 2)
+    return big.reshape(2, 256, 256)
 
 
 def split(x):
@@ -194,13 +194,13 @@
         return c, near
 
     def sweep(copies, body, carry):
-        carry = lax.fori_loop(0, 28, lambda q, c: body(1 + q // 14, 1 + q % 14, c), carry, unroll=2)
+        carry = lax.fori_loop(0, 28, lambda q, c: body(1 + q // 14, 1 + q % 14, c), carry, unroll=4)
         copies[2].wait()
         copies[3].wait()
         carry = lax.fori_loop(0, 4, lambda q, c: body(1 + q // 2, 15 * (q % 2), c), carry)
         copies[0].wait()
         copies[1].wait()
-        return lax.fori_loop(0, 32, lambda q, c: body(3 * (q // 16), q % 16, c), carry, unroll=2)
+        return lax.fori_loop(0, 32, lambda q, c: body(3 * (q // 16), q % 16, c), carry, unroll=4)
 
     class Both:
         def __init__(self, a, b):
@@ -287,6 +287,10 @@
         part = ref.at[j, :, pl.ds(0, LINES)]
         pltpu.make_async_copy(part, part, sem.at[j]).wait()
 
+    def mirrored(piece):
+        piece = pltpu.roll(piece, 4, 1)
+        return jnp.concatenate([piece[i : i + 1] for i in range(NW - 1, -1, -1)], axis=0)
+
     def folded(line):
         return line[:, 0:128] + line[:, 128:256] + line[:, 256:384] + line[:, 384:512]
 
@@ -313,16 +317,20 @@
         table = parts_of(ty_ref)
         u = []
         for zl in range(2):
-            a = jnp.concatenate(
-                [
-                    recvf[j, q * 32 : (q + 1) * 32, zl * 8 : (zl + 1) * 8, :].reshape(256, 128)
-                    for q in range(NN)
-                ],
-                axis=1,
-            )
-            u.append(product(split(a), table, nt))
-        u = jnp.concatenate(u, axis=0)
-        v = product(parts_of(b_ref), split(u), nn)
+            a = []
+            for q in range(NN):
+                piece = recvf[j, q * 32 : (q + 1) * 32, zl * 8 : (zl + 1) * 8, :]
+                if zl == 1:
+                    piece = mirrored(piece)
+                a.append(piece.reshape(256, 128))
+            u.append(product(split(jnp.concatenate(a, axis=1)), table, nt))
+        v = jnp.concatenate(
+            [
+                product((b_ref[0, 0], b_ref[1, 0]), split(u[0] + u[1]), nn),
+                product((b_ref[0, 1], b_ref[1, 1]), split(u[0] - u[1]), nn),
+            ],
+            axis=0,
+        )
         pi = summed(jnp.sum(recvf[j, :, 16:17, :], axis=0))
         alpha = jnp.where(first, -1.0, rho / pi)
         step = jnp.where(first, 0.0, rho / pi)
@@ -331,12 +339,16 @@
         scaled = left * inv_ref[...]
         q_part = jnp.sum(left * scaled, axis=0, keepdims=True)
         sbi[:, 16:17, :] = jnp.broadcast_to(folded(q_part), (ND, 1, 128))
-        back = product(parts_of(bt_ref), split(scaled), nn)
+        even = product((bt_ref[0, 0], bt_ref[1, 0]), split(scaled[0:256]), nn)
+        odd = product((bt_ref[0, 1], bt_ref[1, 1]), split(scaled[256:512]), nn)
         table = parts_of(ty_ref)
         for zl in range(2):
-            r = product(split(back[zl * 256 : (zl + 1) * 256]), table, nn)
+            r = product(split(even - odd if zl == 1 else even + odd), table, nn)
             for q in range(NN):
-                sbi[q * 32 : (q + 1) * 32, zl * 8 : (zl + 1) * 8, :] = r[:, q * 128 : (q + 1) * 128].reshape(32, 8, 128)
+                piece = r[:, q * 128 : (q + 1) * 128].reshape(32, 8, 128)
+                if zl == 1:
+                    piece = mirrored(piece)
+                sbi[q * 32 : (q + 1) * 32, zl * 8 : (zl + 1) * 8, :] = piece
         own = pltpu.make_async_copy(sbi.at[me, sent], recvi.at[j, me, sent], sem_ir.at[j])
         own.start()
         bulk(j, lambda p: sbi.at[p, sent], recvi, sem_is, sem_ir)
@@ -353,25 +365,30 @@
         wait_others(j, recvf, sem_fs)
         wait_all(j, recvi, sem_ir)
         wait_others(j, recvi, sem_is)
-        fresh = summed(jnp.sum(recvi[j, :, 16:17, :], axis=0))
-        mix = jnp.where(first, 0.0, fresh / rho)
-        planes = [[], []]
-        for zl in range(2):
+        def layer(z):
+            zl = z % 2
             got = recvi[j, :, zl * 8 : (zl + 1) * 8, :].reshape(64, 2, 8, 128)
             even, odd = got[:, 0], got[:, 1]
-            planes[0].append(jnp.where(half, even, pltpu.roll(odd, 4, 1)).reshape(ROWS, 128).T)
-            planes[1].append(jnp.where(half, pltpu.roll(even, 4, 1), odd).reshape(ROWS, 128).T)
+            if z < 2:
+                rows = jnp.where(half, even, pltpu.roll(odd, 4, 1))
+            else:
+                rows = jnp.where(half, pltpu.roll(even, 4, 1), odd)
+            return rows.reshape(ROWS, 128).T
+
         table = parts_of(tx_ref)
         field = spad.at[j]
         copies = halo(2 + j, lambda z, y: field.at[(z + 1) if isinstance(z, int) else pl.ds(1, 4), y], 8, lambda z, y: field.at[z, y])
-        for h in range(2):
-            r = product(split(jnp.concatenate(planes[h], axis=0)), table, nn)
-            spad[j, 1 + 2 * h : 3 + 2 * h, 8:136, :] = r.reshape(2, 128, NX)
-            if h == 0:
+        for z in ((0, 3), (1, 2)):
+            r = product(split(jnp.concatenate([layer(q) for q in z], axis=0)), table, nn)
+            spad[j, 1 + z[0], 8:136, :] = r[0:128]
+            spad[j, 1 + z[1], 8:136, :] = r[128:256]
+            if z[0] == 0:
+                copies[0].start()
                 copies[1].start()
-        copies[0].start()
         copies[2].start()
         copies[3].start()
+        fresh = summed(jnp.sum(recvi[j, :, 16:17, :], axis=0))
+        mix = jnp.where(first, 0.0, fresh / rho)
 
         def stencil(z, i, carry):
             rows = pl.ds(pl.multiple_of(8 * (16 * z + i), 8), 8)
@@ -423,20 +440,28 @@
     lax.fori_loop(0, 64, finish, 0, unroll=4)
 
 
+def hand_on(a, b, c, d, e, f):
+    d[...] = a[...]
+    e[...] = b[...]
+    f[...] = c[...]
+
+
 def on_device(temp, phase, table, north, east):
-    ez = np.repeat(eigen_np(NZ) + 0.01, 4).reshape(64, 8, 1).astype(np.float32)
+    ez = np.concatenate([eigen_np(NZ)[0::2], eigen_np(NZ)[1::2]]) + 0.01
+    ez = np.repeat(ez, 4).reshape(64, 8, 1).astype(np.float32)
     ey = eigen_np(NY).astype(np.float32).reshape(1, NY)
     ex = eigen_np(NX).astype(np.float32).reshape(1, NX)
     bz = z_table()
-    tables = [jnp.asarray(split_np(t)) for t in (cosine_np(NX), cosine_np(NY), bz, bz.T)]
+    tables = [jnp.asarray(split_np(t)) for t in (cosine_np(NX), cosine_np(NY), bz, bz.transpose(0, 2, 1))]
     vmem = pl.BlockSpec(memory_space=pltpu.VMEM)
     anywhere = pl.BlockSpec(memory_space=pl.ANY)
     tabled = pltpu.VMEM((2, ROWS, ROWS), BF16)
+    folded = pltpu.VMEM((2, 2, 256, 256), BF16)
     smem = pl.BlockSpec(memory_space=pltpu.SMEM)
     shape = jax.ShapeDtypeStruct((4, 128, NX), F32)
     dma = pltpu.SemaphoreType.DMA
     square = pltpu.VMEM((ROWS, NX), F32)
-    return pl.pallas_call(
+    results = pl.pallas_call(
         whole_kernel,
         out_shape=(shape, shape, shape),
         in_specs=[anywhere, anywhere, smem, vmem, vmem] + [anywhere] * 4 + [vmem] * 3,
@@ -444,8 +469,8 @@
         scratch_shapes=[
             tabled,
             tabled,
-            tabled,
-            tabled,
+            folded,
+            folded,
             pltpu.VMEM((6, 144, NX), F32),
             pltpu.VMEM((6, 144, NX), jnp.int32),
             pltpu.VMEM((ITERS, 6, 144, NX), F32),
@@ -476,6 +501,14 @@
             collective_id=0, has_side_effects=True, vmem_limit_bytes=60 * 2**20
         ),
     )(temp, phase, table.reshape(16), north, east, *tables, jnp.asarray(ez), jnp.asarray(ey), jnp.asarray(ex))
+    layer = pl.BlockSpec((1, 128, NX), lambda z: (z, 0, 0))
+    return pl.pallas_call(
+        hand_on,
+        grid=(4,),
+        out_shape=(shape, shape, shape),
+        in_specs=[layer] * 3,
+        out_specs=(layer, layer, layer),
+    )(*results)
 
 
 def solution(mesh):

time: 173 us -> 168 us (0.971)
  local copies, waits for them, and re-layouts: 4.93 us -> 0 us
    unnamed x7 -> x0, local copies, waits for them, and re-layouts: 4.93 us -> none
    pallas_call x1, Pallas kernels: 166 us -> 162 us  [on_device(): pl.pallas_call(whole_kernel, out_shape=(shape, shape, shape), in_specs=[a...]
    pallas_call x0 -> x1, Pallas kernels: none -> 4.14 us  [on_device(): pl.pallas_call(hand_on, grid=(4,), out_shape=(shape, shape, shape), in_sp...]
where the time goes in v4:
time: 168 us; the launch traced here: 167 us
  Pallas kernels  166 us (99%)
    pallas_call x1, Pallas kernels, on_device(): pl.pallas_call(whole_kernel, out_shape=(shape, shape, shape), in_specs=[a...  162 us
    pallas_call x1, Pallas kernels, on_device(): pl.pallas_call(hand_on, grid=(4,), out_shape=(shape, shape, shape), in_sp...  4.14 us

profile of v4, /device:TPU:0, one launch (start us, length us, event | category | flops | bytes accessed | tf_op | source)
XLA Modules:
  0.0 166.8 jit_solution(559669329378383302)
XLA Ops:
  0.6 162.0 %shard_map.139 = (f32[4,128,512]{2,1,0:T(8,128)}, f32[4,128,512]{2,1,0:T(8,128)}, f32[4,128,512]{2,1,0:T(8,128)}) custom-call(f32[4,128,512]{2,1,0:T(8,128)} %temp_ref.1, s32[4,128,512]{2,1,0:T(8,128)} %phase_ref.1, s32[16]{0:T(128)} %bitcast.1, f32[16,16]{1,0:T(8,128)} %north_ref.1, f32[128,128]{1,0:T(8,128)} %east_ref.1, ...), custom_call_target="tpu_custom_call" | custom-call | tf_op jit(solution)/shard_map/pallas_call | solution.py:464
  162.6 4.1 %shard_map.140 = (f32[4,128,512]{2,1,0:T(8,128)}, f32[4,128,512]{2,1,0:T(8,128)}, f32[4,128,512]{2,1,0:T(8,128)}) custom-call(f32[4,128,512]{2,1,0:T(8,128)} %get-tuple-element.6.a, f32[4,128,512]{2,1,0:T(8,128)} %get-tuple-element.7.b, f32[4,128,512]{2,1,0:T(8,128)} %get-tuple-element.8.c), custom_call_target="tpu_custom_call" | custom-call | tf_op jit(solution)/shard_map/pallas_call | solution.py:505

commit v5 on v4

--- a/solution.py
+++ b/solution.py
@@ -89,10 +89,11 @@
 
 def whole_kernel(
     temp_ref, phase_ref, table_ref, north_ref, east_ref, tx_any, ty_any, b_any, bt_any, ez_ref, ey_ref, ex_ref,
+    tnext_any, press_any, resid_any,
     tnext_ref, press_ref, resid_ref,
     tx_ref, ty_ref, b_ref, bt_ref, tpad, ppad, spad, wts, mass, f_ref, c_ref, d_ref, inv_ref,
     sbf, sbi, recvf, recvi, red_n, red_w,
-    sem_fs, sem_fr, sem_is, sem_ir, sem_rs, sem_rr, sem_hs, sem_hr, sem_ready, sem_load,
+    sem_fs, sem_fr, sem_is, sem_ir, sem_rs, sem_rr, sem_hs, sem_hr, sem_ready, sem_load, sem_store,
 ):
     w = lax.axis_index("wide")
     n = lax.axis_index("narrow")
@@ -233,6 +234,8 @@
         return carry
 
     sweep([Both(head[i], head[4 + i]) for i in range(4)], head_chunk, 0)
+    stores = [pltpu.make_async_copy(tnext_ref, tnext_any, sem_store.at[8])]
+    stores[0].start()
     pl.semaphore_wait(sem_ready, NN - 1)
 
     ra = lax.broadcasted_iota(jnp.int32, (128, 16), 0)
@@ -424,26 +427,60 @@
         pltpu.make_async_copy(part, part, ssem).wait()
         return jnp.sum(slots[...], axis=0)
 
-    red_n[n] = line
-    red_w[w] = gather(red_n, n, NN, lambda step: (w, (n + step) % NN), sem_rs.at[0], sem_rr.at[0])
-    pi = summed(gather(red_w, w, NW, lambda step: ((w + step) % NW, n), sem_rs.at[1], sem_rr.at[1]))
+    y, z, c = w // 8, (w // 2) % 4, w % 2
+    mine = n * 2 + c
+    red_n[mine] = line
+    red_w[w // 2] = gather(
+        red_n, mine, 8, lambda t: (w - c + (c + t) % 2, (n + t // 2) % 4), sem_rs.at[0], sem_rr.at[0]
+    )
+    pi = gather(
+        red_w,
+        w // 2,
+        16,
+        lambda t: (((y + t // 4) % 4) * 8 + ((z + t) % 4) * 2 + c, n),
+        sem_rs.at[1],
+        sem_rr.at[1],
+    )
+    pi = summed(pi)
     alpha = rho / pi
 
-    def finish(g, carry):
-        z, i = g // 16, g % 16
-        rows = pl.ds(pl.multiple_of(8 * g, 8), 8)
-        line = pl.ds(pl.multiple_of(8 * i, 8), 8)
-        press_ref[z, line, :] = press_ref[z, line, :] + alpha * d_ref[rows, :]
-        resid_ref[z, line, :] = resid_ref[z, line, :] - alpha * f_ref[rows, :]
-        return carry
-
-    lax.fori_loop(0, 64, finish, 0, unroll=4)
-
-
-def hand_on(a, b, c, d, e, f):
-    d[...] = a[...]
-    e[...] = b[...]
-    f[...] = c[...]
+    for z in range(4):
+
+        def finish(i, carry):
+            rows = pl.ds(pl.multiple_of(128 * z + 8 * i, 8), 8)
+            line = pl.ds(pl.multiple_of(8 * i, 8), 8)
+            press_ref[z, line, :] = press_ref[z, line, :] + alpha * d_ref[rows, :]
+            resid_ref[z, line, :] = resid_ref[z, line, :] - alpha * f_ref[rows, :]
+            return carry
+
+        lax.fori_loop(0, 16, finish, 0, unroll=4)
+        for i, (a, b) in enumerate(((press_ref, press_any), (resid_ref, resid_any))):
+            stores.append(pltpu.make_async_copy(a.at[z], b.at[z], sem_store.at[2 * z + i]))
+            stores[-1].start()
+    for store in stores:
+        store.wait()
+
+
+def hand_on(a, b, c, d, e, f, held, sem_in, sem_out):
+    moves = []
+    for i, (source, target) in enumerate(((a, d), (b, e), (c, f))):
+        for z in (0, 2):
+            at = pl.ds(z, 2)
+            k = 2 * i + z // 2
+            slot = held.at[k]
+            moves.append(
+                (
+                    pltpu.make_async_copy(source.at[at], slot, sem_in.at[k]),
+                    pltpu.make_async_copy(slot, target.at[at], sem_out.at[k]),
+                )
+            )
+    for load, _ in moves:
+        load.start()
+    for load, store in moves:
+        load.wait()
+        store.start()
+    for _, store in moves:
+        store.wait()
 
 
 def on_device(temp, phase, table, north, east):
@@ -457,6 +494,7 @@
     anywhere = pl.BlockSpec(memory_space=pl.ANY)
     tabled = pltpu.VMEM((2, ROWS, ROWS), BF16)
     folded = pltpu.VMEM((2, 2, 256, 256), BF16)
+    block = pltpu.VMEM((4, 128, NX), F32)
     smem = pl.BlockSpec(memory_space=pltpu.SMEM)
     shape = jax.ShapeDtypeStruct((4, 128, NX), F32)
     dma = pltpu.SemaphoreType.DMA
@@ -465,8 +503,11 @@
         whole_kernel,
         out_shape=(shape, shape, shape),
         in_specs=[anywhere, anywhere, smem, vmem, vmem] + [anywhere] * 4 + [vmem] * 3,
-        out_specs=(vmem, vmem, vmem),
+        out_specs=(anywhere, anywhere, anywhere),
         scratch_shapes=[
+            block,
+            block,
+            block,
             tabled,
             tabled,
             folded,
@@ -484,8 +525,8 @@
             pltpu.VMEM((ND, 24, 128), F32),
             pltpu.VMEM((ITERS, ND, 24, 128), F32),
             pltpu.VMEM((ITERS, ND, 24, 128), F32),
-            pltpu.VMEM((NN, 1, 128), F32),
-            pltpu.VMEM((NW, 1, 128), F32),
+            pltpu.VMEM((8, 1, 128), F32),
+            pltpu.VMEM((16, 1, 128), F32),
             dma((ITERS,)),
             dma((ITERS,)),
             dma((ITERS,)),
@@ -496,18 +537,19 @@
             dma((5, 4)),
             pltpu.SemaphoreType.REGULAR,
             dma((6,)),
+            dma((9,)),
         ],
         compiler_params=pltpu.CompilerParams(
             collective_id=0, has_side_effects=True, vmem_limit_bytes=60 * 2**20
         ),
     )(temp, phase, table.reshape(16), north, east, *tables, jnp.asarray(ez), jnp.asarray(ey), jnp.asarray(ex))
-    layer = pl.BlockSpec((1, 128, NX), lambda z: (z, 0, 0))
     return pl.pallas_call(
         hand_on,
-        grid=(4,),
         out_shape=(shape, shape, shape),
-        in_specs=[layer] * 3,
-        out_specs=(layer, layer, layer),
+        in_specs=[anywhere] * 3,
+        out_specs=(anywhere, anywhere, anywhere),
+        scratch_shapes=[pltpu.VMEM((6, 2, 128, NX), F32), dma((6,)), dma((6,))],
+        compiler_params=pltpu.CompilerParams(vmem_limit_bytes=60 * 2**20),
     )(*results)
 
 

time: 168 us -> 166 us (0.988)
  no operation moved by 1% of the time
where the time goes in v5:
time: 166 us; the launch traced here: 165 us
  Pallas kernels  165 us (99%)
    pallas_call x1, Pallas kernels, on_device(): pl.pallas_call(whole_kernel, out_shape=(shape, shape, shape), in_specs=[a...  162 us

profile of v5, /device:TPU:0, one launch (start us, length us, event | category | flops | bytes accessed | tf_op | source)
XLA Modules:
  0.0 165.4 jit_solution(17873636192307921629)
XLA Ops:
  0.6 162.0 %shard_map.139 = (f32[4,128,512]{2,1,0:T(8,128)}, f32[4,128,512]{2,1,0:T(8,128)}, f32[4,128,512]{2,1,0:T(8,128)}) custom-call(f32[4,128,512]{2,1,0:T(8,128)} %temp_ref.1, s32[4,128,512]{2,1,0:T(8,128)} %phase_ref.1, s32[16]{0:T(128)} %bitcast.1, f32[16,16]{1,0:T(8,128)} %north_ref.1, f32[128,128]{1,0:T(8,128)} %east_ref.1, ...), custom_call_target="tpu_custom_call" | custom-call | tf_op jit(solution)/shard_map/pallas_call | solution.py:502
  162.6 2.8 %shard_map.140 = (f32[4,128,512]{2,1,0:T(8,128)}, f32[4,128,512]{2,1,0:T(8,128)}, f32[4,128,512]{2,1,0:T(8,128)}) custom-call(f32[4,128,512]{2,1,0:T(8,128)} %get-tuple-element.6.a, f32[4,128,512]{2,1,0:T(8,128)} %get-tuple-element.7.b, f32[4,128,512]{2,1,0:T(8,128)} %get-tuple-element.8.c), custom_call_target="tpu_custom_call" | custom-call | tf_op jit(solution)/shard_map/pallas_call | solution.py:546

commit v6 on v5

--- a/solution.py
+++ b/solution.py
@@ -84,7 +84,7 @@
             send(((y + dy) % 4) * 8 + ((z + dz) % 4) * 2 + (c + flip) % 2, (n + dx) % 4)
             return carry
 
-        lax.fori_loop(1 if sum(hops) == 0 else 0, 2 ** (ones + 1), body, 0)
+        lax.fori_loop(1 if sum(hops) == 0 else 0, 2 ** (ones + 1), body, 0, unroll=min(4, 2**ones))
 
 
 def whole_kernel(

time: 166 us -> 165 us (level)
  no operation moved by 1% of the time
where the time goes in v6:
time: 165 us
  Pallas kernels  164 us (99%)
    pallas_call x1, Pallas kernels, on_device(): pl.pallas_call(whole_kernel, out_shape=(shape, shape, shape), in_specs=[a...  162 us

profile of v6, /device:TPU:0, one launch (start us, length us, event | category | flops | bytes accessed | tf_op | source)
XLA Modules:
  0.0 165.0 jit_solution(14157221668999294093)
XLA Ops:
  0.6 161.6 %shard_map.139 = (f32[4,128,512]{2,1,0:T(8,128)}, f32[4,128,512]{2,1,0:T(8,128)}, f32[4,128,512]{2,1,0:T(8,128)}) custom-call(f32[4,128,512]{2,1,0:T(8,128)} %temp_ref.1, s32[4,128,512]{2,1,0:T(8,128)} %phase_ref.1, s32[16]{0:T(128)} %bitcast.1, f32[16,16]{1,0:T(8,128)} %north_ref.1, f32[128,128]{1,0:T(8,128)} %east_ref.1, ...), custom_call_target="tpu_custom_call" | custom-call | tf_op jit(solution)/shard_map/pallas_call | solution.py:502
  162.2 2.8 %shard_map.140 = (f32[4,128,512]{2,1,0:T(8,128)}, f32[4,128,512]{2,1,0:T(8,128)}, f32[4,128,512]{2,1,0:T(8,128)}) custom-call(f32[4,128,512]{2,1,0:T(8,128)} %get-tuple-element.6.a, f32[4,128,512]{2,1,0:T(8,128)} %get-tuple-element.7.b, f32[4,128,512]{2,1,0:T(8,128)} %get-tuple-element.8.c), custom_call_target="tpu_custom_call" | custom-call | tf_op jit(solution)/shard_map/pallas_call | solution.py:546
